TPU v7x, 512 devices: a whole 4x8x8 slice. The times are simulated.
512 devices in a mesh: tm: 8 (over z_lo, core), gz: 64 (over x, z_hi, y).
Axes of the slice: x: 4, y: 8, z: 8 (z_hi: 2, z_lo: 4; z = z_hi * 4 + z_lo), core: 2. Of those that a mesh axis runs over, the one named last changes fastest.
Arguments:
- init_states: float32 [8, 2, 128, 32, 256], P('tm', None, 'gz'), may hold values from 0 to 1
- diffusivity: float32 [128, 32, 256], P('gz'), may hold values from 0.5 to 2
Outputs:
- nodes: float32 [8, 3, 2, 128, 32, 256], P('tm', None, None, 'gz')
All inputs are finite; a program needn't handle non-finite values.
Results may differ from a plain program's by a relative error of at most 0.0001.
Values sent between devices are 32-bit elements; how exact they have to be, the bound alone decides.
A program may use at most 64 MiB of HBM per device.

v0:
```python
import jax
import jax.numpy as jnp
from jax import lax
from jax.sharding import PartitionSpec as P

DIFF_U = 0.16
DIFF_V = 0.08
FEED_RATE = 0.035
KILL_RATE = 0.06
TIME_STEP = 0.8
HALF_STEP = 0.4
WEIGHTS = ((5.0 / 24.0, 1.0 / 3.0, -1.0 / 24.0), (-1.0 / 24.0, 1.0 / 3.0, 5.0 / 24.0))


def extended(block, sides, width):
    for axis, dim in sides:
        count = lax.axis_size(axis)
        forward = [(i, i + 1) for i in range(count - 1)]
        forward.append((count - 1, 0))
        backward = [(target, source) for source, target in forward]
        low = lax.ppermute(
            lax.slice_in_dim(block, block.shape[dim] - width, None, axis=dim), axis, forward
        )
        high = lax.ppermute(lax.slice_in_dim(block, 0, width, axis=dim), axis, backward)
        block = jnp.concatenate([low, block, high], axis=dim)
    return block


def shifted(value, axis, steps):
    count = lax.axis_size(axis)
    initial, last = (max(0, -steps), min(count, count - steps))
    return lax.ppermute(value, axis, [(source, source + steps) for source in range(initial, last)])


def laplace_pad(padded, spacing):
    centre = padded[:, :, 1:-1]
    along_z = padded[:, :, 2:] + padded[:, :, :-2] - 2.0 * centre
    along_x = jnp.roll(centre, 1, 3) + jnp.roll(centre, -1, 3) - 2.0 * centre
    along_y = jnp.roll(centre, 1, 4) + jnp.roll(centre, -1, 4) - 2.0 * centre
    return (centre, along_z + (along_x + along_y) / spacing)


def reaction(padded, diffuse, spacing):
    centre, laplace = laplace_pad(padded, spacing)
    conc_u = centre[:, 0]
    conc_v = centre[:, 1]
    product = conc_u * conc_v * conc_v
    rate_u = DIFF_U * diffuse * laplace[:, 0] - product + FEED_RATE * (1.0 - conc_u)
    rate_v = DIFF_V * diffuse * laplace[:, 1] + product - (FEED_RATE + KILL_RATE) * conc_v
    return jnp.stack([rate_u, rate_v], 1)


def integral(rates, row):
    return TIME_STEP * (
        WEIGHTS[row][0] * rates[0] + WEIGHTS[row][1] * rates[1] + WEIGHTS[row][2] * rates[2]
    )


def coarsen(field):
    shape = field.shape[:-2] + (field.shape[-2] // 2, 2, field.shape[-1] // 2, 2)
    return 0.25 * jnp.sum(field.reshape(shape), axis=(-3, -1))


def refine(field):
    return jnp.repeat(jnp.repeat(field, 2, -2), 2, -1)


def sweep(begin, first_rate, old_rates, consts, evaluate):
    u_one = begin + HALF_STEP * (first_rate - old_rates[0]) + consts[0]
    rate_one = evaluate(u_one)
    u_two = u_one + HALF_STEP * (rate_one - old_rates[1]) + consts[1]
    return (u_one, rate_one, u_two)


def local(init_states, diffusivity):
    slices = lax.axis_size("tm")
    is_first = lax.axis_index("tm") == 0
    initial = init_states[0]
    coarse_diff = coarsen(diffusivity)

    def fine_one(state):
        padded = extended(state[None], (("gz", 2),), 1)
        return reaction(padded, diffusivity, 1.0)[0]

    def coarse_one(state):
        padded = extended(state[None], (("gz", 2),), 1)
        return reaction(padded, coarse_diff, 4.0)[0]

    rate_init = fine_one(initial)
    same = (rate_init, rate_init, rate_init)
    consts = (integral(same, 0), integral(same, 1))
    u_one, rate_one, u_two = sweep(initial, rate_init, same, consts, fine_one)
    rate_two = fine_one(u_two)
    nodes_a = jnp.stack([initial, u_one, u_two])
    rates_a = (rate_init, rate_one, rate_two)
    coarse_old = coarsen(nodes_a)
    padded_old = extended(coarse_old, (("gz", 2),), 1)
    coarse_rates = reaction(padded_old, coarse_diff, 4.0)
    coarse_consts = (coarsen(integral(rates_a, 0)), coarsen(integral(rates_a, 1)))
    begin = coarse_old[0]
    for round_no in range(slices):
        c_one, rate_mid, c_two = sweep(
            begin, coarse_one(begin), coarse_rates, coarse_consts, coarse_one
        )
        c_one, c_two = (c_one, c_two)
        if round_no + 1 < slices:
            received = shifted(c_two, "tm", 1)
            begin = jnp.where(is_first, coarse_old[0], received)
    correction = jnp.stack([begin, c_one, c_two]) - coarse_old
    corrected = nodes_a + refine(correction)
    received_fine = shifted(corrected[2], "tm", 1)
    begin_b = jnp.where(is_first, corrected[0], received_fine)
    padded = extended(corrected, (("gz", 2),), 1)
    old_rates = reaction(padded, diffusivity, 1.0)
    consts_b = (integral(old_rates, 0), integral(old_rates, 1))
    b_one, rate_skip, b_two = sweep(begin_b, fine_one(begin_b), old_rates, consts_b, fine_one)
    return jnp.stack([begin_b, b_one, b_two])[None]


def solution(mesh):
    placed = (P("tm", None, "gz", None, None), P("gz", None, None))
    return jax.shard_map(
        local,
        mesh=mesh,
        in_specs=placed,
        out_specs=P("tm", None, None, "gz", None, None),
        check_vma=False,
    )
```

profile of v0, /device:TPU:1, one launch (start us, length us, event | category | flops | bytes accessed | tf_op | source)
XLA Modules:
  0.0 516.0 jit_solution(13696040277308301651)
XLA Ops:
  4.9 14.5 %collective-permute-start = (f32[1,2,1,32,256]{4,3,2,1,0:T(8,128)S(1)}, f32[1,2,1,32,256]{4,3,2,1,0:T(8,128)S(1)}, u32[]{:S(2)}, u32[]{:S(2)}) collective-permute-start(f32[1,2,1,32,256]{4,3,2,1,0:T(8,128)S(1)} %get-tuple-element.85), channel_id=1, source_target_pairs={{1,0},{2,1},{3,2},{4,3},{5,4},{6,5},{7,6},{8,7},{9,8},{10,9},{11,1... | collective-permute-start | bytes 196616 | tf_op jit(solution)/shard_map/ppermute | solution.py:24
  31.6 9.7 %stack.191 = f32[1,2,2,16,2,128,2]{6,5,4,3,2,1,0:T(8,128)} reshape(f32[1,2,2,32,256]{4,3,2,1,0:T(8,128)S(1)} %copy-done.2) | data formatting | bytes 262144 | tf_op jit(solution)/shard_map/stack | solution.py:94
  49.0 11.5 %collective-permute-start.2 = (f32[1,2,1,32,256]{4,3,2,1,0:T(8,128)S(1)}, f32[1,2,1,32,256]{4,3,2,1,0:T(8,128)S(1)}, u32[]{:S(2)}, u32[]{:S(2)}) collective-permute-start(f32[1,2,1,32,256]{4,3,2,1,0:T(8,128)S(1)} %get-tuple-element.75), channel_id=1, source_target_pairs={{1,0},{2,1},{3,2},{4,3},{5,4},{6,5},{7,6},{8,7},{9,8},{10,9},{11,1... | collective-permute-start | bytes 196616 | tf_op jit(solution)/shard_map/ppermute | solution.py:24
  110.1 11.7 %collective-permute-start.4 = (f32[1,2,1,16,128]{4,3,2,1,0:T(8,128)S(1)}, f32[1,2,1,16,128]{4,3,2,1,0:T(8,128)S(1)}, u32[]{:S(2)}, u32[]{:S(2)}) collective-permute-start(f32[1,2,1,16,128]{4,3,2,1,0:T(8,128)S(1)} %get-tuple-element.105), channel_id=1, source_target_pairs={{1,0},{2,1},{3,2},{4,3},{5,4},{6,5},{7,6},{8,7},{9,8},{10,9},{11,1... | collective-permute-start | bytes 49160 | tf_op jit(solution)/shard_map/ppermute | solution.py:24
  134.8 11.6 %collective-permute-start.8 = (f32[1,2,1,32,256]{4,3,2,1,0:T(8,128)S(1)}, f32[1,2,1,32,256]{4,3,2,1,0:T(8,128)S(1)}, u32[]{:S(2)}, u32[]{:S(2)}) collective-permute-start(f32[1,2,1,32,256]{4,3,2,1,0:T(8,128)S(1)} %get-tuple-element.65), channel_id=1, source_target_pairs={{1,0},{2,1},{3,2},{4,3},{5,4},{6,5},{7,6},{8,7},{9,8},{10,9},{11,1... | collective-permute-start | bytes 196616 | tf_op jit(solution)/shard_map/ppermute | solution.py:24
  154.1 11.5 %collective-permute-start.6 = (f32[3,2,1,16,128]{4,3,2,1,0:T(8,128)S(1)}, f32[3,2,1,16,128]{4,3,2,1,0:T(8,128)S(1)}, u32[]{:S(2)}, u32[]{:S(2)}) collective-permute-start(f32[3,2,1,16,128]{4,3,2,1,0:T(8,128)S(1)} %get-tuple-element.95), channel_id=1, source_target_pairs={{1,0},{2,1},{3,2},{4,3},{5,4},{6,5},{7,6},{8,7},{9,8},{10,9},{11,1... | collective-permute-start | bytes 147464 | tf_op jit(solution)/shard_map/ppermute | solution.py:24
  186.1 12.3 %collective-permute-start.10 = (f32[1,2,1,16,128]{4,3,2,1,0:T(8,128)S(1)}, f32[1,2,1,16,128]{4,3,2,1,0:T(8,128)S(1)}, u32[]{:S(2)}, u32[]{:S(2)}) collective-permute-start(f32[1,2,1,16,128]{4,3,2,1,0:T(8,128)S(1)} %get-tuple-element.287), channel_id=1, source_target_pairs={{1,0},{2,1},{3,2},{4,3},{5,4},{6,5},{7,6},{8,7},{9,8},{10,9},{11,1... | collective-permute-start | bytes 49160 | tf_op jit(solution)/shard_map/ppermute | solution.py:24
  209.9 12.1 %collective-permute-start.13 = (f32[1,2,1,16,128]{4,3,2,1,0:T(8,128)S(1)}, f32[1,2,1,16,128]{4,3,2,1,0:T(8,128)S(1)}, u32[]{:S(2)}, u32[]{:S(2)}) collective-permute-start(f32[1,2,1,16,128]{4,3,2,1,0:T(8,128)S(1)} %get-tuple-element.277), channel_id=1, source_target_pairs={{1,0},{2,1},{3,2},{4,3},{5,4},{6,5},{7,6},{8,7},{9,8},{10,9},{11,1... | collective-permute-start | bytes 49160 | tf_op jit(solution)/shard_map/ppermute | solution.py:24
  225.1 12.2 %collective-permute-start.15 = (f32[1,2,1,16,128]{4,3,2,1,0:T(8,128)S(1)}, f32[1,2,1,16,128]{4,3,2,1,0:T(8,128)S(1)}, u32[]{:S(2)}, u32[]{:S(2)}) collective-permute-start(f32[1,2,1,16,128]{4,3,2,1,0:T(8,128)S(1)} %get-tuple-element.267), channel_id=1, source_target_pairs={{1,0},{2,1},{3,2},{4,3},{5,4},{6,5},{7,6},{8,7},{9,8},{10,9},{11,1... | collective-permute-start | bytes 49160 | tf_op jit(solution)/shard_map/ppermute | solution.py:24
  247.2 12.1 %collective-permute-start.18 = (f32[1,2,1,16,128]{4,3,2,1,0:T(8,128)S(1)}, f32[1,2,1,16,128]{4,3,2,1,0:T(8,128)S(1)}, u32[]{:S(2)}, u32[]{:S(2)}) collective-permute-start(f32[1,2,1,16,128]{4,3,2,1,0:T(8,128)S(1)} %get-tuple-element.257), channel_id=1, source_target_pairs={{1,0},{2,1},{3,2},{4,3},{5,4},{6,5},{7,6},{8,7},{9,8},{10,9},{11,1... | collective-permute-start | bytes 49160 | tf_op jit(solution)/shard_map/ppermute | solution.py:24
  262.3 11.9 %collective-permute-start.20 = (f32[1,2,1,16,128]{4,3,2,1,0:T(8,128)S(1)}, f32[1,2,1,16,128]{4,3,2,1,0:T(8,128)S(1)}, u32[]{:S(2)}, u32[]{:S(2)}) collective-permute-start(f32[1,2,1,16,128]{4,3,2,1,0:T(8,128)S(1)} %get-tuple-element.247), channel_id=1, source_target_pairs={{1,0},{2,1},{3,2},{4,3},{5,4},{6,5},{7,6},{8,7},{9,8},{10,9},{11,1... | collective-permute-start | bytes 49160 | tf_op jit(solution)/shard_map/ppermute | solution.py:24
  284.4 12.1 %collective-permute-start.23 = (f32[1,2,1,16,128]{4,3,2,1,0:T(8,128)S(1)}, f32[1,2,1,16,128]{4,3,2,1,0:T(8,128)S(1)}, u32[]{:S(2)}, u32[]{:S(2)}) collective-permute-start(f32[1,2,1,16,128]{4,3,2,1,0:T(8,128)S(1)} %get-tuple-element.237), channel_id=1, source_target_pairs={{1,0},{2,1},{3,2},{4,3},{5,4},{6,5},{7,6},{8,7},{9,8},{10,9},{11,1... | collective-permute-start | bytes 49160 | tf_op jit(solution)/shard_map/ppermute | solution.py:24
  299.5 11.9 %collective-permute-start.25 = (f32[1,2,1,16,128]{4,3,2,1,0:T(8,128)S(1)}, f32[1,2,1,16,128]{4,3,2,1,0:T(8,128)S(1)}, u32[]{:S(2)}, u32[]{:S(2)}) collective-permute-start(f32[1,2,1,16,128]{4,3,2,1,0:T(8,128)S(1)} %get-tuple-element.227), channel_id=1, source_target_pairs={{1,0},{2,1},{3,2},{4,3},{5,4},{6,5},{7,6},{8,7},{9,8},{10,9},{11,1... | collective-permute-start | bytes 49160 | tf_op jit(solution)/shard_map/ppermute | solution.py:24
  321.6 12.1 %collective-permute-start.28 = (f32[1,2,1,16,128]{4,3,2,1,0:T(8,128)S(1)}, f32[1,2,1,16,128]{4,3,2,1,0:T(8,128)S(1)}, u32[]{:S(2)}, u32[]{:S(2)}) collective-permute-start(f32[1,2,1,16,128]{4,3,2,1,0:T(8,128)S(1)} %get-tuple-element.217), channel_id=1, source_target_pairs={{1,0},{2,1},{3,2},{4,3},{5,4},{6,5},{7,6},{8,7},{9,8},{10,9},{11,1... | collective-permute-start | bytes 49160 | tf_op jit(solution)/shard_map/ppermute | solution.py:24
  336.8 11.9 %collective-permute-start.30 = (f32[1,2,1,16,128]{4,3,2,1,0:T(8,128)S(1)}, f32[1,2,1,16,128]{4,3,2,1,0:T(8,128)S(1)}, u32[]{:S(2)}, u32[]{:S(2)}) collective-permute-start(f32[1,2,1,16,128]{4,3,2,1,0:T(8,128)S(1)} %get-tuple-element.207), channel_id=1, source_target_pairs={{1,0},{2,1},{3,2},{4,3},{5,4},{6,5},{7,6},{8,7},{9,8},{10,9},{11,1... | collective-permute-start | bytes 49160 | tf_op jit(solution)/shard_map/ppermute | solution.py:24
  358.9 12.1 %collective-permute-start.33 = (f32[1,2,1,16,128]{4,3,2,1,0:T(8,128)S(1)}, f32[1,2,1,16,128]{4,3,2,1,0:T(8,128)S(1)}, u32[]{:S(2)}, u32[]{:S(2)}) collective-permute-start(f32[1,2,1,16,128]{4,3,2,1,0:T(8,128)S(1)} %get-tuple-element.197), channel_id=1, source_target_pairs={{1,0},{2,1},{3,2},{4,3},{5,4},{6,5},{7,6},{8,7},{9,8},{10,9},{11,1... | collective-permute-start | bytes 49160 | tf_op jit(solution)/shard_map/ppermute | solution.py:24
  374.0 11.9 %collective-permute-start.35 = (f32[1,2,1,16,128]{4,3,2,1,0:T(8,128)S(1)}, f32[1,2,1,16,128]{4,3,2,1,0:T(8,128)S(1)}, u32[]{:S(2)}, u32[]{:S(2)}) collective-permute-start(f32[1,2,1,16,128]{4,3,2,1,0:T(8,128)S(1)} %get-tuple-element.187), channel_id=1, source_target_pairs={{1,0},{2,1},{3,2},{4,3},{5,4},{6,5},{7,6},{8,7},{9,8},{10,9},{11,1... | collective-permute-start | bytes 49160 | tf_op jit(solution)/shard_map/ppermute | solution.py:24
  396.1 12.1 %collective-permute-start.38 = (f32[1,2,1,16,128]{4,3,2,1,0:T(8,128)S(1)}, f32[1,2,1,16,128]{4,3,2,1,0:T(8,128)S(1)}, u32[]{:S(2)}, u32[]{:S(2)}) collective-permute-start(f32[1,2,1,16,128]{4,3,2,1,0:T(8,128)S(1)} %get-tuple-element.177), channel_id=1, source_target_pairs={{1,0},{2,1},{3,2},{4,3},{5,4},{6,5},{7,6},{8,7},{9,8},{10,9},{11,1... | collective-permute-start | bytes 49160 | tf_op jit(solution)/shard_map/ppermute | solution.py:24
  411.3 11.9 %collective-permute-start.40 = (f32[1,2,1,16,128]{4,3,2,1,0:T(8,128)S(1)}, f32[1,2,1,16,128]{4,3,2,1,0:T(8,128)S(1)}, u32[]{:S(2)}, u32[]{:S(2)}) collective-permute-start(f32[1,2,1,16,128]{4,3,2,1,0:T(8,128)S(1)} %get-tuple-element.167), channel_id=1, source_target_pairs={{1,0},{2,1},{3,2},{4,3},{5,4},{6,5},{7,6},{8,7},{9,8},{10,9},{11,1... | collective-permute-start | bytes 49160 | tf_op jit(solution)/shard_map/ppermute | solution.py:24
  433.4 12.1 %collective-permute-start.43 = (f32[1,2,1,16,128]{4,3,2,1,0:T(8,128)S(1)}, f32[1,2,1,16,128]{4,3,2,1,0:T(8,128)S(1)}, u32[]{:S(2)}, u32[]{:S(2)}) collective-permute-start(f32[1,2,1,16,128]{4,3,2,1,0:T(8,128)S(1)} %get-tuple-element.157), channel_id=1, source_target_pairs={{1,0},{2,1},{3,2},{4,3},{5,4},{6,5},{7,6},{8,7},{9,8},{10,9},{11,1... | collective-permute-start | bytes 49160 | tf_op jit(solution)/shard_map/ppermute | solution.py:24
  448.5 12.2 %collective-permute-start.45 = (f32[1,2,1,16,128]{4,3,2,1,0:T(8,128)S(1)}, f32[1,2,1,16,128]{4,3,2,1,0:T(8,128)S(1)}, u32[]{:S(2)}, u32[]{:S(2)}) collective-permute-start(f32[1,2,1,16,128]{4,3,2,1,0:T(8,128)S(1)} %get-tuple-element.147), channel_id=1, source_target_pairs={{1,0},{2,1},{3,2},{4,3},{5,4},{6,5},{7,6},{8,7},{9,8},{10,9},{11,1... | collective-permute-start | bytes 49160 | tf_op jit(solution)/shard_map/ppermute | solution.py:24
  471.3 12.1 %collective-permute-start.50 = (f32[3,2,1,32,256]{4,3,2,1,0:T(8,128)S(1)}, f32[3,2,1,32,256]{4,3,2,1,0:T(8,128)S(1)}, u32[]{:S(2)}, u32[]{:S(2)}) collective-permute-start(f32[3,2,1,32,256]{4,3,2,1,0:T(8,128)S(1)} %get-tuple-element.21), channel_id=1, source_target_pairs={{1,0},{2,1},{3,2},{4,3},{5,4},{6,5},{7,6},{8,7},{9,8},{10,9},{11,1... | collective-permute-start | bytes 589832 | tf_op jit(solution)/shard_map/ppermute | solution.py:24
  485.6 11.5 %collective-permute-start.48 = (f32[1,2,1,32,256]{4,3,2,1,0:T(8,128)S(1)}, f32[1,2,1,32,256]{4,3,2,1,0:T(8,128)S(1)}, u32[]{:S(2)}, u32[]{:S(2)}) collective-permute-start(f32[1,2,1,32,256]{4,3,2,1,0:T(8,128)S(1)} %get-tuple-element.55), channel_id=1, source_target_pairs={{1,0},{2,1},{3,2},{4,3},{5,4},{6,5},{7,6},{8,7},{9,8},{10,9},{11,1... | collective-permute-start | bytes 196616 | tf_op jit(solution)/shard_map/ppermute | solution.py:24
  501.3 12.4 %collective-permute-start.52 = (f32[1,2,1,32,256]{4,3,2,1,0:T(8,128)S(1)}, f32[1,2,1,32,256]{4,3,2,1,0:T(8,128)S(1)}, u32[]{:S(2)}, u32[]{:S(2)}) collective-permute-start(f32[1,2,1,32,256]{4,3,2,1,0:T(8,128)S(1)} %get-tuple-element.45), channel_id=1, source_target_pairs={{1,0},{2,1},{3,2},{4,3},{5,4},{6,5},{7,6},{8,7},{9,8},{10,9},{11,1... | collective-permute-start | bytes 196616 | tf_op jit(solution)/shard_map/ppermute | solution.py:24
  (315 shorter events, 227.4 us)
Async XLA Ops:
  0.9 45.7 %collective-permute-start.1 = (f32[1,2,1,32,256]{4,3,2,1,0:T(8,128)S(1)}, f32[1,2,1,32,256]{4,3,2,1,0:T(8,128)S(1)}, u32[]{:S(2)}, u32[]{:S(2)}) collective-permute-start(f32[1,2,1,32,256]{4,3,2,1,0:T(8,128)S(1)} %get-tuple-element.86), channel_id=1, source_target_pairs={{0,1},{1,2},{2,3},{3,4},{4,5},{5,6},{6,7},{7,8},{8,9},{9,10},{10,1... | collective-permute-start | bytes 196616 | tf_op jit(solution)/shard_map/ppermute | solution.py:21
  4.9 41.7 %collective-permute-start = (f32[1,2,1,32,256]{4,3,2,1,0:T(8,128)S(1)}, f32[1,2,1,32,256]{4,3,2,1,0:T(8,128)S(1)}, u32[]{:S(2)}, u32[]{:S(2)}) collective-permute-start(f32[1,2,1,32,256]{4,3,2,1,0:T(8,128)S(1)} %get-tuple-element.85), channel_id=1, source_target_pairs={{1,0},{2,1},{3,2},{4,3},{5,4},{6,5},{7,6},{8,7},{9,8},{10,9},{11,1... | collective-permute-start | bytes 196616 | tf_op jit(solution)/shard_map/ppermute | solution.py:24
  47.1 45.1 %collective-permute-start.3 = (f32[1,2,1,32,256]{4,3,2,1,0:T(8,128)S(1)}, f32[1,2,1,32,256]{4,3,2,1,0:T(8,128)S(1)}, u32[]{:S(2)}, u32[]{:S(2)}) collective-permute-start(f32[1,2,1,32,256]{4,3,2,1,0:T(8,128)S(1)} %get-tuple-element.76), channel_id=1, source_target_pairs={{0,1},{1,2},{2,3},{3,4},{4,5},{5,6},{6,7},{7,8},{8,9},{9,10},{10,1... | collective-permute-start | bytes 196616 | tf_op jit(solution)/shard_map/ppermute | solution.py:21
  49.0 43.2 %collective-permute-start.2 = (f32[1,2,1,32,256]{4,3,2,1,0:T(8,128)S(1)}, f32[1,2,1,32,256]{4,3,2,1,0:T(8,128)S(1)}, u32[]{:S(2)}, u32[]{:S(2)}) collective-permute-start(f32[1,2,1,32,256]{4,3,2,1,0:T(8,128)S(1)} %get-tuple-element.75), channel_id=1, source_target_pairs={{1,0},{2,1},{3,2},{4,3},{5,4},{6,5},{7,6},{8,7},{9,8},{10,9},{11,1... | collective-permute-start | bytes 196616 | tf_op jit(solution)/shard_map/ppermute | solution.py:24
  108.2 45.9 %collective-permute-start.5 = (f32[1,2,1,16,128]{4,3,2,1,0:T(8,128)S(1)}, f32[1,2,1,16,128]{4,3,2,1,0:T(8,128)S(1)}, u32[]{:S(2)}, u32[]{:S(2)}) collective-permute-start(f32[1,2,1,16,128]{4,3,2,1,0:T(8,128)S(1)} %get-tuple-element.106), channel_id=1, source_target_pairs={{0,1},{1,2},{2,3},{3,4},{4,5},{5,6},{6,7},{7,8},{8,9},{9,10},{10,1... | collective-permute-start | bytes 49160 | tf_op jit(solution)/shard_map/ppermute | solution.py:21
  110.1 55.5 %collective-permute-start.4 = (f32[1,2,1,16,128]{4,3,2,1,0:T(8,128)S(1)}, f32[1,2,1,16,128]{4,3,2,1,0:T(8,128)S(1)}, u32[]{:S(2)}, u32[]{:S(2)}) collective-permute-start(f32[1,2,1,16,128]{4,3,2,1,0:T(8,128)S(1)} %get-tuple-element.105), channel_id=1, source_target_pairs={{1,0},{2,1},{3,2},{4,3},{5,4},{6,5},{7,6},{8,7},{9,8},{10,9},{11,1... | collective-permute-start | bytes 49160 | tf_op jit(solution)/shard_map/ppermute | solution.py:24
  132.9 34.0 %collective-permute-start.9 = (f32[1,2,1,32,256]{4,3,2,1,0:T(8,128)S(1)}, f32[1,2,1,32,256]{4,3,2,1,0:T(8,128)S(1)}, u32[]{:S(2)}, u32[]{:S(2)}) collective-permute-start(f32[1,2,1,32,256]{4,3,2,1,0:T(8,128)S(1)} %get-tuple-element.66), channel_id=1, source_target_pairs={{0,1},{1,2},{2,3},{3,4},{4,5},{5,6},{6,7},{7,8},{8,9},{9,10},{10,1... | collective-permute-start | bytes 196616 | tf_op jit(solution)/shard_map/ppermute | solution.py:21
  134.8 32.1 %collective-permute-start.8 = (f32[1,2,1,32,256]{4,3,2,1,0:T(8,128)S(1)}, f32[1,2,1,32,256]{4,3,2,1,0:T(8,128)S(1)}, u32[]{:S(2)}, u32[]{:S(2)}) collective-permute-start(f32[1,2,1,32,256]{4,3,2,1,0:T(8,128)S(1)} %get-tuple-element.65), channel_id=1, source_target_pairs={{1,0},{2,1},{3,2},{4,3},{5,4},{6,5},{7,6},{8,7},{9,8},{10,9},{11,1... | collective-permute-start | bytes 196616 | tf_op jit(solution)/shard_map/ppermute | solution.py:24
  184.2 14.3 %collective-permute-start.11 = (f32[1,2,1,16,128]{4,3,2,1,0:T(8,128)S(1)}, f32[1,2,1,16,128]{4,3,2,1,0:T(8,128)S(1)}, u32[]{:S(2)}, u32[]{:S(2)}) collective-permute-start(f32[1,2,1,16,128]{4,3,2,1,0:T(8,128)S(1)} %get-tuple-element.288), channel_id=1, source_target_pairs={{0,1},{1,2},{2,3},{3,4},{4,5},{5,6},{6,7},{7,8},{8,9},{9,10},{10,1... | collective-permute-start | bytes 49160 | tf_op jit(solution)/shard_map/ppermute | solution.py:21
  208.0 14.0 %collective-permute-start.14 = (f32[1,2,1,16,128]{4,3,2,1,0:T(8,128)S(1)}, f32[1,2,1,16,128]{4,3,2,1,0:T(8,128)S(1)}, u32[]{:S(2)}, u32[]{:S(2)}) collective-permute-start(f32[1,2,1,16,128]{4,3,2,1,0:T(8,128)S(1)} %get-tuple-element.278), channel_id=1, source_target_pairs={{0,1},{1,2},{2,3},{3,4},{4,5},{5,6},{6,7},{7,8},{8,9},{9,10},{10,1... | collective-permute-start | bytes 49160 | tf_op jit(solution)/shard_map/ppermute | solution.py:21
  223.1 14.2 %collective-permute-start.16 = (f32[1,2,1,16,128]{4,3,2,1,0:T(8,128)S(1)}, f32[1,2,1,16,128]{4,3,2,1,0:T(8,128)S(1)}, u32[]{:S(2)}, u32[]{:S(2)}) collective-permute-start(f32[1,2,1,16,128]{4,3,2,1,0:T(8,128)S(1)} %get-tuple-element.268), channel_id=1, source_target_pairs={{0,1},{1,2},{2,3},{3,4},{4,5},{5,6},{6,7},{7,8},{8,9},{9,10},{10,1... | collective-permute-start | bytes 49160 | tf_op jit(solution)/shard_map/ppermute | solution.py:21
  245.2 14.0 %collective-permute-start.19 = (f32[1,2,1,16,128]{4,3,2,1,0:T(8,128)S(1)}, f32[1,2,1,16,128]{4,3,2,1,0:T(8,128)S(1)}, u32[]{:S(2)}, u32[]{:S(2)}) collective-permute-start(f32[1,2,1,16,128]{4,3,2,1,0:T(8,128)S(1)} %get-tuple-element.258), channel_id=1, source_target_pairs={{0,1},{1,2},{2,3},{3,4},{4,5},{5,6},{6,7},{7,8},{8,9},{9,10},{10,1... | collective-permute-start | bytes 49160 | tf_op jit(solution)/shard_map/ppermute | solution.py:21
  260.4 13.9 %collective-permute-start.21 = (f32[1,2,1,16,128]{4,3,2,1,0:T(8,128)S(1)}, f32[1,2,1,16,128]{4,3,2,1,0:T(8,128)S(1)}, u32[]{:S(2)}, u32[]{:S(2)}) collective-permute-start(f32[1,2,1,16,128]{4,3,2,1,0:T(8,128)S(1)} %get-tuple-element.248), channel_id=1, source_target_pairs={{0,1},{1,2},{2,3},{3,4},{4,5},{5,6},{6,7},{7,8},{8,9},{9,10},{10,1... | collective-permute-start | bytes 49160 | tf_op jit(solution)/shard_map/ppermute | solution.py:21
  282.5 14.0 %collective-permute-start.24 = (f32[1,2,1,16,128]{4,3,2,1,0:T(8,128)S(1)}, f32[1,2,1,16,128]{4,3,2,1,0:T(8,128)S(1)}, u32[]{:S(2)}, u32[]{:S(2)}) collective-permute-start(f32[1,2,1,16,128]{4,3,2,1,0:T(8,128)S(1)} %get-tuple-element.238), channel_id=1, source_target_pairs={{0,1},{1,2},{2,3},{3,4},{4,5},{5,6},{6,7},{7,8},{8,9},{9,10},{10,1... | collective-permute-start | bytes 49160 | tf_op jit(solution)/shard_map/ppermute | solution.py:21
  319.7 14.0 %collective-permute-start.29 = (f32[1,2,1,16,128]{4,3,2,1,0:T(8,128)S(1)}, f32[1,2,1,16,128]{4,3,2,1,0:T(8,128)S(1)}, u32[]{:S(2)}, u32[]{:S(2)}) collective-permute-start(f32[1,2,1,16,128]{4,3,2,1,0:T(8,128)S(1)} %get-tuple-element.218), channel_id=1, source_target_pairs={{0,1},{1,2},{2,3},{3,4},{4,5},{5,6},{6,7},{7,8},{8,9},{9,10},{10,1... | collective-permute-start | bytes 49160 | tf_op jit(solution)/shard_map/ppermute | solution.py:21
  357.0 14.0 %collective-permute-start.34 = (f32[1,2,1,16,128]{4,3,2,1,0:T(8,128)S(1)}, f32[1,2,1,16,128]{4,3,2,1,0:T(8,128)S(1)}, u32[]{:S(2)}, u32[]{:S(2)}) collective-permute-start(f32[1,2,1,16,128]{4,3,2,1,0:T(8,128)S(1)} %get-tuple-element.198), channel_id=1, source_target_pairs={{0,1},{1,2},{2,3},{3,4},{4,5},{5,6},{6,7},{7,8},{8,9},{9,10},{10,1... | collective-permute-start | bytes 49160 | tf_op jit(solution)/shard_map/ppermute | solution.py:21
  372.1 13.9 %collective-permute-start.36 = (f32[1,2,1,16,128]{4,3,2,1,0:T(8,128)S(1)}, f32[1,2,1,16,128]{4,3,2,1,0:T(8,128)S(1)}, u32[]{:S(2)}, u32[]{:S(2)}) collective-permute-start(f32[1,2,1,16,128]{4,3,2,1,0:T(8,128)S(1)} %get-tuple-element.188), channel_id=1, source_target_pairs={{0,1},{1,2},{2,3},{3,4},{4,5},{5,6},{6,7},{7,8},{8,9},{9,10},{10,1... | collective-permute-start | bytes 49160 | tf_op jit(solution)/shard_map/ppermute | solution.py:21
  394.2 14.0 %collective-permute-start.39 = (f32[1,2,1,16,128]{4,3,2,1,0:T(8,128)S(1)}, f32[1,2,1,16,128]{4,3,2,1,0:T(8,128)S(1)}, u32[]{:S(2)}, u32[]{:S(2)}) collective-permute-start(f32[1,2,1,16,128]{4,3,2,1,0:T(8,128)S(1)} %get-tuple-element.178), channel_id=1, source_target_pairs={{0,1},{1,2},{2,3},{3,4},{4,5},{5,6},{6,7},{7,8},{8,9},{9,10},{10,1... | collective-permute-start | bytes 49160 | tf_op jit(solution)/shard_map/ppermute | solution.py:21
  431.4 14.0 %collective-permute-start.44 = (f32[1,2,1,16,128]{4,3,2,1,0:T(8,128)S(1)}, f32[1,2,1,16,128]{4,3,2,1,0:T(8,128)S(1)}, u32[]{:S(2)}, u32[]{:S(2)}) collective-permute-start(f32[1,2,1,16,128]{4,3,2,1,0:T(8,128)S(1)} %get-tuple-element.158), channel_id=1, source_target_pairs={{0,1},{1,2},{2,3},{3,4},{4,5},{5,6},{6,7},{7,8},{8,9},{9,10},{10,1... | collective-permute-start | bytes 49160 | tf_op jit(solution)/shard_map/ppermute | solution.py:21
  446.6 14.2 %collective-permute-start.46 = (f32[1,2,1,16,128]{4,3,2,1,0:T(8,128)S(1)}, f32[1,2,1,16,128]{4,3,2,1,0:T(8,128)S(1)}, u32[]{:S(2)}, u32[]{:S(2)}) collective-permute-start(f32[1,2,1,16,128]{4,3,2,1,0:T(8,128)S(1)} %get-tuple-element.148), channel_id=1, source_target_pairs={{0,1},{1,2},{2,3},{3,4},{4,5},{5,6},{6,7},{7,8},{8,9},{9,10},{10,1... | collective-permute-start | bytes 49160 | tf_op jit(solution)/shard_map/ppermute | solution.py:21
  463.3 20.0 %collective-permute-start.47 = (f32[2,2,32,256]{3,2,1,0:T(8,128)S(1)}, f32[2,2,32,256]{3,2,1,0:T(8,128)S(1)}, u32[]{:S(2)}, u32[]{:S(2)}) collective-permute-start(f32[2,2,32,256]{3,2,1,0:T(8,128)S(1)} %slice_bitcast_fusion.8), channel_id=1, source_target_pairs={{0,64},{64,128},{128,192},{192,256},{256,320},{320,384},{384,448},... | collective-permute-start | bytes 393224 | tf_op jit(solution)/shard_map/ppermute | solution.py:32
  469.4 29.2 %collective-permute-start.51 = (f32[3,2,1,32,256]{4,3,2,1,0:T(8,128)S(1)}, f32[3,2,1,32,256]{4,3,2,1,0:T(8,128)S(1)}, u32[]{:S(2)}, u32[]{:S(2)}) collective-permute-start(f32[3,2,1,32,256]{4,3,2,1,0:T(8,128)S(1)} %get-tuple-element.22), channel_id=1, source_target_pairs={{0,1},{1,2},{2,3},{3,4},{4,5},{5,6},{6,7},{7,8},{8,9},{9,10},{10,1... | collective-permute-start | bytes 589832 | tf_op jit(solution)/shard_map/ppermute | solution.py:21
  471.3 27.3 %collective-permute-start.50 = (f32[3,2,1,32,256]{4,3,2,1,0:T(8,128)S(1)}, f32[3,2,1,32,256]{4,3,2,1,0:T(8,128)S(1)}, u32[]{:S(2)}, u32[]{:S(2)}) collective-permute-start(f32[3,2,1,32,256]{4,3,2,1,0:T(8,128)S(1)} %get-tuple-element.21), channel_id=1, source_target_pairs={{1,0},{2,1},{3,2},{4,3},{5,4},{6,5},{7,6},{8,7},{9,8},{10,9},{11,1... | collective-permute-start | bytes 589832 | tf_op jit(solution)/shard_map/ppermute | solution.py:24
  499.3 14.3 %collective-permute-start.53 = (f32[1,2,1,32,256]{4,3,2,1,0:T(8,128)S(1)}, f32[1,2,1,32,256]{4,3,2,1,0:T(8,128)S(1)}, u32[]{:S(2)}, u32[]{:S(2)}) collective-permute-start(f32[1,2,1,32,256]{4,3,2,1,0:T(8,128)S(1)} %get-tuple-element.46), channel_id=1, source_target_pairs={{0,1},{1,2},{2,3},{3,4},{4,5},{5,6},{6,7},{7,8},{8,9},{9,10},{10,1... | collective-permute-start | bytes 196616 | tf_op jit(solution)/shard_map/ppermute | solution.py:21
  (35 other events, 453.3 us)
where the time goes:
time: 518 us; the launch traced here: 516 us
  starting transfers between devices  373 us (72%)
  local copies, waits for them, and re-layouts  111 us (21%)
  waiting for transfers between devices  22.8 us (4%)
  other arithmetic  7.59 us (1%)
    ppermute x23, starting transfers between devices, extended(): lax.ppermute(lax.slice_in_dim(block, 0, width, axis=dim), axis, backward)  277 us
    another operation x12, local copies, waits for them, and re-layouts, reaction(): return jnp.stack([rate_u, rate_v], 1)  50.3 us
    ppermute x8, starting transfers between devices, shifted(): lax.ppermute(value, axis, [(source, source + steps) for source in range(i...  49.6 us
    ppermute x23, starting transfers between devices, extended(): lax.ppermute(lax.slice_in_dim(block, block.shape[dim] - width, None, axis...  46.2 us
    another operation x6, local copies, waits for them, and re-layouts, local(): nodes_a = jnp.stack([initial, u_one, u_two])  44.8 us
    ppermute x23, waiting for transfers between devices, extended(): lax.ppermute(lax.slice_in_dim(block, 0, width, axis=dim), axis, backward)  15.4 us
  transfers between devices with their start and end apart: 54, of which 26 were waited for; matrix products, arithmetic and copies ran while one was open for 15% of the time, Pallas kernels for 0%

commit v1 on v0

v1 whole, which is shorter than its diff:
```python
import jax
import jax.numpy as jnp
from jax import lax
from jax.experimental import pallas as pl
from jax.experimental.pallas import tpu as pltpu
from jax.sharding import PartitionSpec as P


MESH = pl.DeviceIdType.MESH
F32 = jnp.float32
STEP = 0.4
W_ONE = (0.8 * 5.0 / 24.0, 0.8 / 3.0, -0.8 / 24.0)
W_TWO = (-0.8 / 24.0, 0.8 / 3.0, 0.8 * 5.0 / 24.0)

CONSTS = (
    (0, 0, 6), (1, 0, 4), (2, 0, 2), (3, 0, 0), (3, 3, 2), (4, 7, 8), (5, 7, 6), (6, 7, 4), (7, 7, 2), (4, 5, 4), (5, 5, 2),
)
WIDTHS = (8, 6, 4, 2, 0)
RUNS = {8: (7,), 6: (0, 7), 4: (0, 5, 7), 2: (0, 3, 5, 7), 0: (0,)}
COARSE_REACH = {0: 3, 3: 2, 5: 3, 7: 5}
MID = 10


def span(k):
    return [0] + [s * i for i in range(1, k + 1) for s in (1, -1)]


def sides(k):
    return span(k)[1:]


def pairs():
    out = set()
    for t in range(8):
        out |= {(t, t, j) for j in sides(2)}
        if t:
            out |= {(t - 1, t, j) for j in span(1)}
    for t, reach in COARSE_REACH.items():
        out |= {(t, t, j) for j in sides(reach)}
    for src, dst, h in CONSTS:
        out |= {(src, dst, j) for j in span(h // 2 + 1) if src != dst or j}
    out |= {(0, 3, j) for j in span(2)} | {(0, 5, j) for j in span(3)} | {(0, 7, j) for j in span(5)}
    out |= {(0, 1, 0), (0, 2, 0), (5, 4, 0), (7, 6, 0)}
    return sorted(out)


def get(ref, *at):
    return [[ref[(*at, s, p)] for p in range(4)] for s in range(2)]


def get_coarse(ref, *at):
    return [ref[(*at, s)] for s in range(2)]


def react(u, v, lap_u, lap_v, du):
    uvv = u * v * v
    return du * lap_u - uvv + 0.035 * (1.0 - u), (0.5 * du) * lap_v + uvv - 0.095 * v


def fine_rate(low, mid, high, du):
    laps = []
    for s in range(2):
        row = []
        for p in range(4):
            across = mid[s][p ^ 2]
            along = mid[s][p ^ 1]
            xs = across + pltpu.roll(across, 15 if p & 2 else 1, 0)
            ys = along + pltpu.roll(along, 127 if p & 1 else 1, 1)
            row.append((low[s][p] + high[s][p]) + (xs + ys) - 6.0 * mid[s][p])
        laps.append(row)
    both = [react(mid[0][p], mid[1][p], laps[0][p], laps[1][p], du[p]) for p in range(4)]
    return [[b[s] for b in both] for s in range(2)]


def coarse_rate(low, mid, high, du):
    laps = []
    for s in range(2):
        c = mid[s]
        xs = pltpu.roll(c, 1, 0) + pltpu.roll(c, 15, 0)
        ys = pltpu.roll(c, 1, 1) + pltpu.roll(c, 127, 1)
        laps.append((low[s] + high[s]) + 0.25 * (xs + ys) - 3.0 * c)
    return react(mid[0], mid[1], laps[0], laps[1], du)


def average(parts):
    return 0.25 * ((parts[0] + parts[1]) + (parts[2] + parts[3]))


def loop(count, body, chunk=1):
    def many(k, carry):
        for i in range(chunk):
            body(k * chunk + i)
        return carry

    lax.fori_loop(0, count // chunk, many, 0)


def swap(forward):
    rows = lax.broadcasted_iota(jnp.int32, (256, 256), 0)
    cols = lax.broadcasted_iota(jnp.int32, (256, 256), 1)
    if not forward:
        rows, cols = cols, rows
    return jnp.where(rows == 2 * (cols % 128) + cols // 128, 1.0, 0.0).astype(F32)


def kernel(
    init, diff, out, xin, din, tmp, woven, a0, a1, a2, ap, du, cd, v0, v1, r0, r1, r2, own, base, one, two,
    d8, d6, d4, d2, d0, b10, b8, b6, b4, b2, b0, w8, w6, w4, w2, w0, dummy,
    in_sem, near_s, near_r, cd_s, cd_r, far_s, far_r, prev_s, prev_r, const_s, const_r, state_s, state_r, give_s, give_r,
):
    tm = lax.axis_index("tm")
    gz = lax.axis_index("gz")
    count = lax.axis_size("gz")
    const = {8: d8, 6: d6, 4: d4, 2: d2, 0: d0}
    state = {10: b10, 8: b8, 6: b6, 4: b4, 2: b2, 0: b0}
    middle = {8: w8, 6: w6, 4: w4, 2: w2, 0: w0}

    def at(t, j):
        return {"tm": t, "gz": lax.rem(gz + (j + count), count)}

    def send(src, dst, ssem, rsem, t, j):
        pltpu.make_async_remote_copy(
            src_ref=src, dst_ref=dst, send_sem=ssem, recv_sem=rsem, device_id=at(t, j), device_id_type=MESH
        ).start()

    def wait(sem, units):
        ref = dummy.at[pl.ds(0, units)]
        pltpu.make_async_copy(ref, ref, sem).wait()

    def on(*slices):
        cond = tm == slices[0]
        for t in slices[1:]:
            cond = cond | (tm == t)
        return pl.when(cond)

    load_x = pltpu.make_async_copy(init.at[0], xin, in_sem.at[0])
    load_d = pltpu.make_async_copy(diff, din, in_sem.at[1])
    load_x.start()
    load_d.start()
    barrier = pltpu.get_barrier_semaphore()
    met = pairs()
    for t in range(8):
        @on(t)
        def _(t=t):
            for src, dst, j in met:
                if dst == t:
                    pl.semaphore_signal(barrier, inc=1, device_id=at(src, -j), device_id_type=MESH)

    order = swap(True)
    load_x.wait()
    load_d.wait()

    def split(rows):
        return jnp.dot(rows, order, precision=lax.Precision.HIGHEST, preferred_element_type=F32)

    mixed = split(xin[...].reshape(128, 256)).reshape(4, 32, 256)
    mixed_d = split(din[...].reshape(64, 256)).reshape(2, 32, 256)
    for half in range(2):
        tmp[half, 0:4] = mixed[:, :, half * 128 : half * 128 + 128]
        tmp[half, 4:6] = mixed_d[:, :, half * 128 : half * 128 + 128]
    for layer in range(2):
        for p in range(4):
            rows = pl.ds(p // 2, 16, stride=2)
            for s in range(2):
                a0[3 + layer, s, p] = tmp[p % 2, s * 2 + layer, rows, :]
            du[2 + layer, p] = 0.16 * tmp[p % 2, 4 + layer, rows, :]
        cd[MID + layer] = average([du[2 + layer, p] for p in range(4)])

    greetings = sum(jnp.where(tm == t, sum(src == t for src, _, _ in met), 0) for t in range(8))
    pl.semaphore_wait(barrier, greetings)

    two_own = pl.ds(3, 2)
    send(a0.at[two_own], a0.at[pl.ds(1, 2)], near_s, near_r, tm, 1)
    send(a0.at[two_own], a0.at[pl.ds(5, 2)], near_s, near_r, tm, -1)
    send(a0.at[4], a0.at[0], near_s, near_r, tm, 2)
    send(a0.at[3], a0.at[7], near_s, near_r, tm, -2)
    send(du.at[pl.ds(2, 2)], du.at[pl.ds(0, 2)], near_s, near_r, tm, 1)
    send(du.at[pl.ds(2, 2)], du.at[pl.ds(4, 2)], near_s, near_r, tm, -1)
    for t, reach in COARSE_REACH.items():
        @on(t)
        def _(t=t, reach=reach):
            for j in sides(reach):
                send(cd.at[pl.ds(MID, 2)], cd.at[pl.ds(MID - 2 * j, 2)], cd_s, cd_r, t, j)
    wait(near_r, 32)

    def first(i):
        c = get(a0, i + 1)
        f = fine_rate(get(a0, i), c, get(a0, i + 2), [du[i, p] for p in range(4)])
        for s in range(2):
            for p in range(4):
                a1[i, s, p] = c[s][p] + STEP * f[s][p]
            r0[i, s] = average(f[s])
            v0[i, s] = average(c[s])

    loop(6, first)

    def second(i):
        c = get(a1, i + 1)
        f = fine_rate(get(a1, i), c, get(a1, i + 2), [du[i + 1, p] for p in range(4)])
        for s in range(2):
            for p in range(4):
                a2[i + 1, s, p] = c[s][p] + STEP * f[s][p]
            r1[i, s] = average(f[s])
            v1[i + 1, s] = average(c[s])

    loop(4, second)

    def third(i):
        f = fine_rate(get(a2, i + 1), get(a2, i + 2), get(a2, i + 3), [du[i + 2, p] for p in range(4)])
        for s in range(2):
            r2[i, s] = average(f[s])

    loop(2, third)

    is_first = jnp.where(tm == 0, 1.0, 0.0).astype(F32)
    for i in range(2):
        g_zero = coarse_rate(get_coarse(v0, i + 1), get_coarse(v0, i + 2), get_coarse(v0, i + 3), cd[MID + i])
        g_one = coarse_rate(get_coarse(v1, i + 1), get_coarse(v1, i + 2), get_coarse(v1, i + 3), cd[MID + i])
        for s in range(2):
            rates = (r0[i + 2, s], r1[i + 1, s], r2[i, s])
            c_zero = W_ONE[0] * rates[0] + W_ONE[1] * rates[1] + W_ONE[2] * rates[2]
            c_one = W_TWO[0] * rates[0] + W_TWO[1] * rates[1] + W_TWO[2] * rates[2]
            own[i, 0, s] = c_zero + is_first * v0[i + 2, s] - (1.0 - is_first) * (STEP * g_zero[s])
            own[i, 1, s] = c_one - STEP * g_one[s]

    for k, (src, dst, h) in enumerate(CONSTS):
        @on(src)
        def _(k=k, src=src, dst=dst, h=h):
            ref = const[h]
            sems = (const_s.at[k], const_r.at[h // 2])
            for j in reversed(span(h // 2)):
                here = pl.ds(h + 1 - 2 * j, 2)
                if src == dst and j == 0:
                    ref[here] = own[...]
                else:
                    send(own, ref.at[here], *sems, dst, j)
            j = h // 2 + 1
            send(own.at[1, 0], ref.at[0, 0], *sems, dst, j)
            send(own.at[0, 0], ref.at[2 * h + 3, 0], *sems, dst, -j)

    send(a2.at[2], a2.at[0], far_s, far_r, tm, 1)
    send(a2.at[3], a2.at[5], far_s, far_r, tm, -1)

    @pl.when(tm < 7)
    def _():
        for j in span(1):
            send(a2.at[pl.ds(2, 2)], ap.at[pl.ds(2 - 2 * j, 2)], prev_s, prev_r, tm + 1, j)

    def prepare():
        wait(far_r, 8)

        @pl.when(tm > 0)
        def _():
            wait(prev_r, 24)

        def body(i):
            for k, (ref, shift) in enumerate(((a0, 1), (a1, 0), (a2, 0), (ap, 0))):
                c = get(ref, i + shift)
                for s in range(2):
                    v = average(c[s])
                    for p in range(4):
                        base[k, i, s, p] = c[s][p] - v

        def body_first(i):
            for k, (ref, shift) in enumerate(((a0, 1), (a1, 0), (a2, 0))):
                c = get(ref, i + shift)
                for s in range(2):
                    v = average(c[s])
                    for p in range(4):
                        base[k, i, s, p] = c[s][p] - v

        @pl.when(tm > 0)
        def _():
            loop(6, body)

        @pl.when(tm == 0)
        def _():
            loop(6, body_first)

    @pl.when(tm > 0)
    def _():
        prepare()

    for t, reach in COARSE_REACH.items():
        @on(t)
        def _(reach=reach):
            wait(cd_r, 2 * reach)

    @on(3)
    def _():
        wait(state_r, 10)

    @on(5)
    def _():
        wait(state_r, 14)

    @on(7)
    def _():
        wait(state_r, 22)

    chunks = {20: 4, 18: 6, 16: 4, 14: 7, 12: 4, 10: 5, 8: 4, 6: 6, 4: 4, 2: 2}

    for h in WIDTHS:
        begin, mid, end, e = state[h + 2], middle[h], state[h], const[h]

        @on(*RUNS[h])
        def _(h=h, begin=begin, mid=mid, end=end, e=e):
            for src, dst, width in CONSTS:
                if width == h:
                    @on(dst)
                    def _(src=src, dst=dst):
                        wait(const_r.at[h // 2], 4 * h + 6 - (4 if src == dst else 0))

            def half(i):
                g = coarse_rate(get_coarse(begin, i), get_coarse(begin, i + 1), get_coarse(begin, i + 2), cd[MID + i - h - 1])
                for s in range(2):
                    mid[i, s] = begin[i + 1, s] + STEP * g[s] + e[i, 0, s]

            def given(i):
                for s in range(2):
                    mid[i, s] = e[i, 0, s]

            def full(i):
                g = coarse_rate(get_coarse(mid, i), get_coarse(mid, i + 1), get_coarse(mid, i + 2), cd[MID + i - h])
                for s in range(2):
                    end[i, s] = mid[i + 1, s] + STEP * g[s] + e[i + 1, 1, s]

            if h == 6:
                @pl.when(tm == 0)
                def _():
                    loop(2 * h + 4, given, 4)

                @pl.when(tm > 0)
                def _():
                    loop(2 * h + 4, half, chunks[2 * h + 4])
            else:
                loop(2 * h + 4, half, chunks[2 * h + 4])
            loop(2 * h + 2, full, chunks[2 * h + 2])

        def give(dst):
            for k, (src_ref, start, dst_ref, to) in enumerate(
                ((state[h + 2], h, b4, 2), (middle[h], h - 1, w2, 1), (state[h], h - 2, b2, 0))
            ):
                send(src_ref.at[pl.ds(start, 6)], dst_ref.at[pl.ds(to, 6)], give_s, give_r, dst, 0)

        if h == 4:
            @on(0)
            def _():
                give(1)

            @on(5, 7)
            def _():
                give(tm - 1)

        if h == 2:
            @on(0)
            def _():
                for j in span(2):
                    send(b2.at[pl.ds(2, 2)], b4.at[pl.ds(4 - 2 * j, 2)], state_s, state_r, 3, j)

        if h == 0:
            @on(0)
            def _():
                for j in reversed(span(5)):
                    send(b0, b10.at[pl.ds(10 - 2 * j, 2)], state_s, state_r, 7, j)
                for j in reversed(span(3)):
                    send(b0, b6.at[pl.ds(6 - 2 * j, 2)], state_s, state_r, 5, j)
                wait(give_s, 18)
                for src_ref, start in ((b4, 2), (w2, 1), (b2, 0)):
                    send(src_ref.at[pl.ds(start, 6)], src_ref.at[pl.ds(start, 6)], give_s, give_r, 2, 0)

    @pl.when(tm == 0)
    def _():
        prepare()

    @on(1, 2, 4, 6)
    def _():
        wait(give_r, 18)

    def correct(zero, zero_at, one_ref, one_at, two_ref, two_at, start):
        def body(i):
            for k, (ref, shift) in enumerate(((zero, zero_at), (one_ref, one_at), (two_ref, two_at))):
                for s in range(2):
                    w = ref[i + shift, s]
                    for p in range(4):
                        base[k, i, s, p] = base[k, i, s, p] + w
                        if k == 0:
                            if start:
                                base[3, i, s, p] = a0[i + 1, s, p]
                            else:
                                base[3, i, s, p] = base[3, i, s, p] + w

        loop(6, body)

    @pl.when(tm == 0)
    def _():
        correct(v0, 0, w6, 5, b6, 4, True)

    @pl.when(tm > 0)
    def _():
        correct(b4, 2, w2, 1, b2, 0, False)

    def fourth(i):
        d = [du[i + 1, p] for p in range(4)]
        f = [fine_rate(get(base, k, i), get(base, k, i + 1), get(base, k, i + 2), d) for k in range(4)]
        for s in range(2):
            for p in range(4):
                rates = [f[k][s][p] for k in range(3)]
                i_one = W_ONE[0] * rates[0] + W_ONE[1] * rates[1] + W_ONE[2] * rates[2]
                i_two = W_TWO[0] * rates[0] + W_TWO[1] * rates[1] + W_TWO[2] * rates[2]
                b_one = base[3, i + 1, s, p] + STEP * (f[3][s][p] - rates[0]) + i_one
                one[i, s, p] = b_one
                two[i, s, p] = b_one - STEP * rates[1] + i_two

    loop(4, fourth)

    def fifth(i):
        f = fine_rate(get(one, i), get(one, i + 1), get(one, i + 2), [du[i + 2, p] for p in range(4)])
        for s in range(2):
            for p in range(4):
                two[i + 1, s, p] = two[i + 1, s, p] + STEP * f[s][p]

    loop(2, fifth)

    back = swap(False)
    for node, (ref, shift) in enumerate(((base.at[3], 2), (one, 1), (two, 1))):
        rows = []
        for s in range(2):
            for layer in range(2):
                for half in range(2):
                    rows.append(
                        jnp.concatenate([ref[shift + layer, s, 2 * half], ref[shift + layer, s, 2 * half + 1]], axis=1)
                    )
        whole = jnp.dot(jnp.concatenate(rows, 0), back, precision=lax.Precision.HIGHEST, preferred_element_type=F32)
        for s in range(2):
            for layer in range(2):
                for side in range(2):
                    lanes = slice(side * 128, side * 128 + 128)
                    for half in range(2):
                        k = (s * 2 + layer) * 2 + half
                        woven[node, s, layer, side, pl.ds(half, 16, stride=2), :] = whole[k * 16 : k * 16 + 16, lanes]
                    out[0, node, s, layer, :, lanes] = woven[node, s, layer, side]

    wait(near_s, 32)
    wait(far_s, 8)
    for t, reach in COARSE_REACH.items():
        @on(t)
        def _(reach=reach):
            wait(cd_s, 2 * reach)

    @pl.when(tm < 7)
    def _():
        wait(prev_s, 24)

    for k, (src, dst, h) in enumerate(CONSTS):
        @on(src)
        def _(k=k, src=src, dst=dst, h=h):
            wait(const_s.at[k], 4 * h + 6 - (4 if src == dst else 0))

    @on(0)
    def _():
        wait(state_s, 46)

    @on(0, 5, 7)
    def _():
        wait(give_s, 18)


def local(init_states, diffusivity):
    fine = (2, 4, 16, 128)
    coarse = (2, 16, 128)

    def vm(*shape):
        return pltpu.VMEM(shape, F32)

    scratch = [vm(2, 2, 32, 256), vm(2, 32, 256), vm(2, 6, 32, 128), vm(3, 2, 2, 2, 32, 128)]
    scratch += [vm(8, *fine), vm(6, *fine), vm(6, *fine), vm(6, *fine), vm(6, 4, 16, 128), vm(2 * MID + 2, 16, 128)]
    scratch += [vm(6, *coarse), vm(6, *coarse), vm(6, *coarse), vm(4, *coarse), vm(2, *coarse), vm(2, 2, *coarse)]
    scratch += [vm(4, 6, *fine), vm(4, *fine), vm(4, *fine)]
    scratch += [vm(2 * h + 4, 2, *coarse) for h in WIDTHS]
    scratch += [vm(2 * h + 2, *coarse) for h in (10,) + WIDTHS]
    scratch += [vm(2 * h + 4, *coarse) for h in WIDTHS]
    scratch += [vm(48, *coarse)]
    dma = pltpu.SemaphoreType.DMA
    one = [dma(()), dma(())]
    scratch += [dma((2,))] + one * 4 + [dma((len(CONSTS),)), dma((5,))] + one * 2
    return pl.pallas_call(
        kernel,
        out_shape=jax.ShapeDtypeStruct((1, 3, 2, 2, 32, 256), F32),
        in_specs=[pl.BlockSpec(memory_space=pl.ANY)] * 2,
        out_specs=pl.BlockSpec(memory_space=pltpu.VMEM),
        scratch_shapes=scratch,
        name="pfasst",
        compiler_params=pltpu.CompilerParams(
            collective_id=0, has_side_effects=True, vmem_limit_bytes=32 * 1024 * 1024
        ),
    )(init_states, diffusivity)


def solution(mesh):
    placed = (P("tm", None, "gz", None, None), P("gz", None, None))
    return jax.shard_map(
        local,
        mesh=mesh,
        in_specs=placed,
        out_specs=P("tm", None, None, "gz", None, None),
        check_vma=False,
    )
```

time: 518 us -> 65.2 us (0.13)
  the two profiles are of different devices: /device:TPU:1 before, /device:TPU:128 now
where the time goes in v1:
time: 65.2 us; the launch traced here: 65 us
  Pallas kernels  62.5 us (96%)
  local copies, waits for them, and re-layouts  2.49 us (4%)
    pallas_call x1, Pallas kernels, local(): pl.pallas_call(kernel, out_shape=jax.ShapeDtypeStruct((1, 3, 2, 2, 32, 25...  62.5 us
    unnamed x5, local copies, waits for them, and re-layouts  2.49 us

profile of v1, /device:TPU:128, one launch (start us, length us, event | category | flops | bytes accessed | tf_op | source)
XLA Modules:
  0.0 65.0 jit_solution(15703864293726970793)
XLA Ops:
  0.0 0.0 copy-start
  0.0 0.9 %copy-done = f32[1,2,2,32,256]{4,3,2,1,0:T(8,128)S(1)} copy-done((f32[1,2,2,32,256]{4,3,2,1,0:T(8,128)S(1)}, f32[1,2,2,32,256]{4,3,2,1,0:T(8,128)}, u32[]{:S(2)}) %copy-start) | copy-done | bytes 131096
  0.9 0.0 copy-start.1
  0.9 0.8 %copy-done.1 = f32[2,32,256]{2,1,0:T(8,128)S(1)} copy-done((f32[2,32,256]{2,1,0:T(8,128)S(1)}, f32[2,32,256]{2,1,0:T(8,128)}, u32[]{:S(2)}) %copy-start.1) | copy-done | bytes 65560
  1.7 62.5 %pfasst.1 = f32[1,3,2,2,32,256]{5,4,3,2,1,0:T(8,128)S(1)} custom-call(f32[1,2,2,32,256]{4,3,2,1,0:T(8,128)S(1)} %copy-done, f32[2,32,256]{2,1,0:T(8,128)S(1)} %copy-done.1), custom_call_target="tpu_custom_call" | custom-call | tf_op jit(solution)/shard_map/pfasst/pallas_call | solution.py:487
  64.3 0.7 %copy.4 = f32[1,3,2,2,32,256]{5,4,3,2,1,0:T(8,128)} copy(f32[1,3,2,2,32,256]{5,4,3,2,1,0:T(8,128)S(1)} %pfasst.1) | data formatting | bytes 786432
Async XLA Ops:
  0.0 0.9 %copy-start = (f32[1,2,2,32,256]{4,3,2,1,0:T(8,128)S(1)}, f32[1,2,2,32,256]{4,3,2,1,0:T(8,128)}, u32[]{:S(2)}) copy-start(f32[1,2,2,32,256]{4,3,2,1,0:T(8,128)} %init.1) | copy-start | bytes 393220
  0.9 0.8 %copy-start.1 = (f32[2,32,256]{2,1,0:T(8,128)S(1)}, f32[2,32,256]{2,1,0:T(8,128)}, u32[]{:S(2)}) copy-start(f32[2,32,256]{2,1,0:T(8,128)} %diff.1) | copy-start | bytes 196612

commit v2 on v1

--- a/solution.py
+++ b/solution.py
@@ -32,11 +32,12 @@
 def pairs():
     out = set()
     for t in range(8):
-        out |= {(t, t, j) for j in sides(2)}
+        out |= {(t, t, j) for j in sides(1)}
+        out.add((t, t ^ 1, 0))
         if t:
-            out |= {(t - 1, t, j) for j in span(1)}
+            out.add((t - 1, t, 0))
     for t, reach in COARSE_REACH.items():
-        out |= {(t, t, j) for j in sides(reach)}
+        out |= {(t, t, j) for j in sides(reach) if abs(j) > 1}
     for src, dst, h in CONSTS:
         out |= {(src, dst, j) for j in span(h // 2 + 1) if src != dst or j}
     out |= {(0, 3, j) for j in span(2)} | {(0, 5, j) for j in span(3)} | {(0, 7, j) for j in span(5)}
@@ -106,7 +107,7 @@
 def kernel(
     init, diff, out, xin, din, tmp, woven, a0, a1, a2, ap, du, cd, v0, v1, r0, r1, r2, own, base, one, two,
     d8, d6, d4, d2, d0, b10, b8, b6, b4, b2, b0, w8, w6, w4, w2, w0, dummy,
-    in_sem, near_s, near_r, cd_s, cd_r, far_s, far_r, prev_s, prev_r, const_s, const_r, state_s, state_r, give_s, give_r,
+    in_sem, near_s, near_r, diff_s, diff_r, cd_s, cd_r, far_s, far_r, prev_s, prev_r, const_s, const_r, state_s, state_r, give_s, give_r,
 ):
     tm = lax.axis_index("tm")
     gz = lax.axis_index("gz")
@@ -164,24 +165,39 @@
             for s in range(2):
                 a0[3 + layer, s, p] = tmp[p % 2, s * 2 + layer, rows, :]
             du[2 + layer, p] = 0.16 * tmp[p % 2, 4 + layer, rows, :]
-        cd[MID + layer] = average([du[2 + layer, p] for p in range(4)])
 
     greetings = sum(jnp.where(tm == t, sum(src == t for src, _, _ in met), 0) for t in range(8))
     pl.semaphore_wait(barrier, greetings)
 
-    two_own = pl.ds(3, 2)
-    send(a0.at[two_own], a0.at[pl.ds(1, 2)], near_s, near_r, tm, 1)
-    send(a0.at[two_own], a0.at[pl.ds(5, 2)], near_s, near_r, tm, -1)
-    send(a0.at[4], a0.at[0], near_s, near_r, tm, 2)
-    send(a0.at[3], a0.at[7], near_s, near_r, tm, -2)
-    send(du.at[pl.ds(2, 2)], du.at[pl.ds(0, 2)], near_s, near_r, tm, 1)
-    send(du.at[pl.ds(2, 2)], du.at[pl.ds(4, 2)], near_s, near_r, tm, -1)
-    for t, reach in COARSE_REACH.items():
-        @on(t)
-        def _(t=t, reach=reach):
-            for j in sides(reach):
-                send(cd.at[pl.ds(MID, 2)], cd.at[pl.ds(MID - 2 * j, 2)], cd_s, cd_r, t, j)
-    wait(near_r, 32)
+    odd = lax.rem(tm, 2)
+    turn = 1 - 2 * odd
+    side = pl.ds(4 * odd, 2)
+    send(a0.at[4], a0.at[2], near_s.at[0], near_r.at[0], tm, 1)
+    send(a0.at[3], a0.at[5], near_s.at[1], near_r.at[1], tm, -1)
+    send(du.at[pl.ds(2, 2)], du.at[side], diff_s.at[0], diff_r.at[0], tm, turn)
+    send(a0.at[3], a0.at[1], near_s.at[2], near_r.at[2], tm, 1)
+    send(a0.at[4], a0.at[6], near_s.at[3], near_r.at[3], tm, -1)
+    wait(near_r.at[0], 4)
+    send(a0.at[2], a0.at[0], near_s.at[4], near_r.at[4], tm, 1)
+    wait(near_r.at[1], 4)
+    send(a0.at[5], a0.at[7], near_s.at[5], near_r.at[5], tm, -1)
+    wait(diff_r.at[0], 4)
+    send(du.at[side], du.at[side], diff_s.at[1], diff_r.at[1], tm + turn, 0)
+    wait(diff_r.at[1], 4)
+    for i in range(6):
+        cd[MID - 2 + i] = average([du[i, p] for p in range(4)])
+
+    def spread(slices):
+        for t in slices:
+            @on(t)
+            def _(t=t):
+                for j in sides(COARSE_REACH[t]):
+                    if abs(j) > 1:
+                        send(cd.at[pl.ds(MID, 2)], cd.at[pl.ds(MID - 2 * j, 2)], cd_s, cd_r, t, j)
+
+    spread((0, 3))
+    wait(near_r.at[2], 4)
+    wait(near_r.at[3], 4)
 
     def first(i):
         c = get(a0, i + 1)
@@ -192,7 +208,7 @@
             r0[i, s] = average(f[s])
             v0[i, s] = average(c[s])
 
-    loop(6, first)
+    loop(4, lambda i: first(i + 1))
 
     def second(i):
         c = get(a1, i + 1)
@@ -203,7 +219,11 @@
             r1[i, s] = average(f[s])
             v1[i + 1, s] = average(c[s])
 
-    loop(4, second)
+    loop(2, lambda i: second(i + 1))
+    wait(near_r.at[4], 4)
+    wait(near_r.at[5], 4)
+    loop(2, lambda i: first(5 * i))
+    loop(2, lambda i: second(3 * i))
 
     def third(i):
         f = fine_rate(get(a2, i + 1), get(a2, i + 2), get(a2, i + 3), [du[i + 2, p] for p in range(4)])
@@ -223,32 +243,39 @@
             own[i, 0, s] = c_zero + is_first * v0[i + 2, s] - (1.0 - is_first) * (STEP * g_zero[s])
             own[i, 1, s] = c_one - STEP * g_one[s]
 
-    for k, (src, dst, h) in enumerate(CONSTS):
-        @on(src)
-        def _(k=k, src=src, dst=dst, h=h):
-            ref = const[h]
-            sems = (const_s.at[k], const_r.at[h // 2])
-            for j in reversed(span(h // 2)):
-                here = pl.ds(h + 1 - 2 * j, 2)
-                if src == dst and j == 0:
-                    ref[here] = own[...]
-                else:
-                    send(own, ref.at[here], *sems, dst, j)
-            j = h // 2 + 1
-            send(own.at[1, 0], ref.at[0, 0], *sems, dst, j)
-            send(own.at[0, 0], ref.at[2 * h + 3, 0], *sems, dst, -j)
-
+    def share():
+        for k, (src, dst, h) in enumerate(CONSTS):
+            @on(src)
+            def _(k=k, src=src, dst=dst, h=h):
+                ref = const[h]
+                sems = (const_s.at[k], const_r.at[h // 2])
+                for j in reversed(span(h // 2)):
+                    here = pl.ds(h + 1 - 2 * j, 2)
+                    if src == dst and j == 0:
+                        ref[here] = own[...]
+                    else:
+                        send(own, ref.at[here], *sems, dst, j)
+                j = h // 2 + 1
+                send(own.at[1, 0], ref.at[0, 0], *sems, dst, j)
+                send(own.at[0, 0], ref.at[2 * h + 3, 0], *sems, dst, -j)
+
+    spread((5, 7))
+    share()
     send(a2.at[2], a2.at[0], far_s, far_r, tm, 1)
     send(a2.at[3], a2.at[5], far_s, far_r, tm, -1)
 
-    @pl.when(tm < 7)
-    def _():
-        for j in span(1):
-            send(a2.at[pl.ds(2, 2)], ap.at[pl.ds(2 - 2 * j, 2)], prev_s, prev_r, tm + 1, j)
+    def pass_on():
+        wait(far_r, 8)
+
+        @pl.when(tm < 7)
+        def _():
+            send(a2, ap, prev_s, prev_r, tm + 1, 0)
+
+    @pl.when(tm > 0)
+    def _():
+        pass_on()
 
     def prepare():
-        wait(far_r, 8)
-
         @pl.when(tm > 0)
         def _():
             wait(prev_r, 24)
@@ -284,7 +311,7 @@
     for t, reach in COARSE_REACH.items():
         @on(t)
         def _(reach=reach):
-            wait(cd_r, 2 * reach)
+            wait(cd_r, 2 * reach - 2)
 
     @on(3)
     def _():
@@ -371,6 +398,7 @@
 
     @pl.when(tm == 0)
     def _():
+        pass_on()
         prepare()
 
     @on(1, 2, 4, 6)
@@ -441,12 +469,15 @@
                         woven[node, s, layer, side, pl.ds(half, 16, stride=2), :] = whole[k * 16 : k * 16 + 16, lanes]
                     out[0, node, s, layer, :, lanes] = woven[node, s, layer, side]
 
-    wait(near_s, 32)
+    for k in range(6):
+        wait(near_s.at[k], 4)
+    for k in range(2):
+        wait(diff_s.at[k], 4)
     wait(far_s, 8)
     for t, reach in COARSE_REACH.items():
         @on(t)
         def _(reach=reach):
-            wait(cd_s, 2 * reach)
+            wait(cd_s, 2 * reach - 2)
 
     @pl.when(tm < 7)
     def _():
@@ -483,11 +514,11 @@
     scratch += [vm(48, *coarse)]
     dma = pltpu.SemaphoreType.DMA
     one = [dma(()), dma(())]
-    scratch += [dma((2,))] + one * 4 + [dma((len(CONSTS),)), dma((5,))] + one * 2
+    scratch += [dma((2,)), dma((6,)), dma((6,)), dma((2,)), dma((2,))] + one * 3 + [dma((len(CONSTS),)), dma((5,))] + one * 2
     return pl.pallas_call(
         kernel,
         out_shape=jax.ShapeDtypeStruct((1, 3, 2, 2, 32, 256), F32),
-        in_specs=[pl.BlockSpec(memory_space=pl.ANY)] * 2,
+        in_specs=[pl.BlockSpec(memory_space=pltpu.HBM)] * 2,
         out_specs=pl.BlockSpec(memory_space=pltpu.VMEM),
         scratch_shapes=scratch,
         name="pfasst",

time: 65.2 us -> 61.8 us (0.948)
  Pallas kernels: 62.5 us -> 59.1 us
    pallas_call x1, Pallas kernels: 62.5 us -> 59.1 us  [local(): pl.pallas_call(kernel, out_shape=jax.ShapeDtypeStruct((1, 3, 2, 2, 32, 25...]
where the time goes in v2:
time: 61.8 us; the launch traced here: 61.6 us
  Pallas kernels  59.1 us (96%)
  local copies, waits for them, and re-layouts  2.49 us (4%)
    pallas_call x1, Pallas kernels, local(): pl.pallas_call(kernel, out_shape=jax.ShapeDtypeStruct((1, 3, 2, 2, 32, 25...  59.1 us
    unnamed x5, local copies, waits for them, and re-layouts  2.49 us

profile of v2, /device:TPU:128, one launch (start us, length us, event | category | flops | bytes accessed | tf_op | source)
XLA Modules:
  0.0 61.6 jit_solution(7887632025789674987)
XLA Ops:
  0.0 0.0 copy-start
  0.0 0.9 %copy-done = f32[1,2,2,32,256]{4,3,2,1,0:T(8,128)S(1)} copy-done((f32[1,2,2,32,256]{4,3,2,1,0:T(8,128)S(1)}, f32[1,2,2,32,256]{4,3,2,1,0:T(8,128)}, u32[]{:S(2)}) %copy-start) | copy-done | bytes 131096
  0.9 0.0 copy-start.1
  0.9 0.8 %copy-done.1 = f32[2,32,256]{2,1,0:T(8,128)S(1)} copy-done((f32[2,32,256]{2,1,0:T(8,128)S(1)}, f32[2,32,256]{2,1,0:T(8,128)}, u32[]{:S(2)}) %copy-start.1) | copy-done | bytes 65560
  1.7 59.1 %pfasst.1 = f32[1,3,2,2,32,256]{5,4,3,2,1,0:T(8,128)S(1)} custom-call(f32[1,2,2,32,256]{4,3,2,1,0:T(8,128)S(1)} %copy-done, f32[2,32,256]{2,1,0:T(8,128)S(1)} %copy-done.1), custom_call_target="tpu_custom_call" | custom-call | tf_op jit(solution)/shard_map/pfasst/pallas_call | solution.py:518
  60.8 0.7 %copy.4 = f32[1,3,2,2,32,256]{5,4,3,2,1,0:T(8,128)} copy(f32[1,3,2,2,32,256]{5,4,3,2,1,0:T(8,128)S(1)} %pfasst.1) | data formatting | bytes 786432
Async XLA Ops:
  0.0 0.9 %copy-start = (f32[1,2,2,32,256]{4,3,2,1,0:T(8,128)S(1)}, f32[1,2,2,32,256]{4,3,2,1,0:T(8,128)}, u32[]{:S(2)}) copy-start(f32[1,2,2,32,256]{4,3,2,1,0:T(8,128)} %init.1) | copy-start | bytes 393220
  0.9 0.8 %copy-start.1 = (f32[2,32,256]{2,1,0:T(8,128)S(1)}, f32[2,32,256]{2,1,0:T(8,128)}, u32[]{:S(2)}) copy-start(f32[2,32,256]{2,1,0:T(8,128)} %diff.1) | copy-start | bytes 196612

commit v3 on v2

--- a/solution.py
+++ b/solution.py
@@ -42,7 +42,7 @@
         out |= {(src, dst, j) for j in span(h // 2 + 1) if src != dst or j}
     out |= {(0, 3, j) for j in span(2)} | {(0, 5, j) for j in span(3)} | {(0, 7, j) for j in span(5)}
     out |= {(0, 1, 0), (0, 2, 0), (5, 4, 0), (7, 6, 0)}
-    return sorted(out)
+    return sorted(out, key=lambda p: (p[0] != p[1] or abs(p[2]) > 1, p))
 
 
 def get(ref, *at):
@@ -97,11 +97,22 @@
 
 
 def swap(forward):
-    rows = lax.broadcasted_iota(jnp.int32, (256, 256), 0)
-    cols = lax.broadcasted_iota(jnp.int32, (256, 256), 1)
-    if not forward:
-        rows, cols = cols, rows
-    return jnp.where(rows == 2 * (cols % 128) + cols // 128, 1.0, 0.0).astype(F32)
+    shape = (256, 128) if forward else (128, 256)
+    whole = lax.broadcasted_iota(jnp.int32, shape, 0 if forward else 1)
+    twice = 2 * lax.broadcasted_iota(jnp.int32, shape, 1 if forward else 0)
+    parts = [jnp.where(whole == twice + p, 1.0, 0.0) for p in range(2)]
+    return jnp.concatenate(parts, axis=1 if forward else 0).astype(jnp.bfloat16)
+
+
+def permute(rows, order):
+    total = None
+    for k in range(3):
+        part = rows.astype(jnp.bfloat16)
+        moved = jnp.dot(part, order, preferred_element_type=F32)
+        total = moved if total is None else total + moved
+        if k < 2:
+            rows = rows - part.astype(F32)
+    return total
 
 
 def kernel(
@@ -151,11 +162,8 @@
     load_x.wait()
     load_d.wait()
 
-    def split(rows):
-        return jnp.dot(rows, order, precision=lax.Precision.HIGHEST, preferred_element_type=F32)
-
-    mixed = split(xin[...].reshape(128, 256)).reshape(4, 32, 256)
-    mixed_d = split(din[...].reshape(64, 256)).reshape(2, 32, 256)
+    mixed = permute(xin[...].reshape(128, 256), order).reshape(4, 32, 256)
+    mixed_d = permute(din[...].reshape(64, 256), order).reshape(2, 32, 256)
     for half in range(2):
         tmp[half, 0:4] = mixed[:, :, half * 128 : half * 128 + 128]
         tmp[half, 4:6] = mixed_d[:, :, half * 128 : half * 128 + 128]
@@ -174,11 +182,22 @@
     side = pl.ds(4 * odd, 2)
     send(a0.at[4], a0.at[2], near_s.at[0], near_r.at[0], tm, 1)
     send(a0.at[3], a0.at[5], near_s.at[1], near_r.at[1], tm, -1)
-    send(du.at[pl.ds(2, 2)], du.at[side], diff_s.at[0], diff_r.at[0], tm, turn)
-    send(a0.at[3], a0.at[1], near_s.at[2], near_r.at[2], tm, 1)
-    send(a0.at[4], a0.at[6], near_s.at[3], near_r.at[3], tm, -1)
+
+    @pl.when(tm < 4)
+    def _():
+        send(du.at[pl.ds(2, 2)], du.at[side], diff_s.at[0], diff_r.at[0], tm, turn)
+        send(a0.at[3], a0.at[1], near_s.at[2], near_r.at[2], tm, 1)
+        send(a0.at[4], a0.at[6], near_s.at[3], near_r.at[3], tm, -1)
+
     wait(near_r.at[0], 4)
     send(a0.at[2], a0.at[0], near_s.at[4], near_r.at[4], tm, 1)
+
+    @pl.when(tm > 3)
+    def _():
+        send(du.at[pl.ds(2, 2)], du.at[side], diff_s.at[0], diff_r.at[0], tm, turn)
+        send(a0.at[3], a0.at[1], near_s.at[2], near_r.at[2], tm, 1)
+        send(a0.at[4], a0.at[6], near_s.at[3], near_r.at[3], tm, -1)
+
     wait(near_r.at[1], 4)
     send(a0.at[5], a0.at[7], near_s.at[5], near_r.at[5], tm, -1)
     wait(diff_r.at[0], 4)
@@ -208,7 +227,7 @@
             r0[i, s] = average(f[s])
             v0[i, s] = average(c[s])
 
-    loop(4, lambda i: first(i + 1))
+    loop(4, lambda i: first(i + 1), 2)
 
     def second(i):
         c = get(a1, i + 1)
@@ -219,18 +238,18 @@
             r1[i, s] = average(f[s])
             v1[i + 1, s] = average(c[s])
 
-    loop(2, lambda i: second(i + 1))
+    loop(2, lambda i: second(i + 1), 2)
     wait(near_r.at[4], 4)
     wait(near_r.at[5], 4)
-    loop(2, lambda i: first(5 * i))
-    loop(2, lambda i: second(3 * i))
+    loop(2, lambda i: first(5 * i), 2)
+    loop(2, lambda i: second(3 * i), 2)
 
     def third(i):
         f = fine_rate(get(a2, i + 1), get(a2, i + 2), get(a2, i + 3), [du[i + 2, p] for p in range(4)])
         for s in range(2):
             r2[i, s] = average(f[s])
 
-    loop(2, third)
+    loop(2, third, 2)
 
     is_first = jnp.where(tm == 0, 1.0, 0.0).astype(F32)
     for i in range(2):
@@ -325,7 +344,7 @@
     def _():
         wait(state_r, 22)
 
-    chunks = {20: 4, 18: 6, 16: 4, 14: 7, 12: 4, 10: 5, 8: 4, 6: 6, 4: 4, 2: 2}
+    chunks = {20: 10, 18: 9, 16: 8, 14: 7, 12: 6, 10: 10, 8: 8, 6: 6, 4: 4, 2: 2}
 
     for h in WIDTHS:
         begin, mid, end, e = state[h + 2], middle[h], state[h], const[h]
@@ -448,7 +467,7 @@
             for p in range(4):
                 two[i + 1, s, p] = two[i + 1, s, p] + STEP * f[s][p]
 
-    loop(2, fifth)
+    loop(2, fifth, 2)
 
     back = swap(False)
     for node, (ref, shift) in enumerate(((base.at[3], 2), (one, 1), (two, 1))):
@@ -459,7 +478,7 @@
                     rows.append(
                         jnp.concatenate([ref[shift + layer, s, 2 * half], ref[shift + layer, s, 2 * half + 1]], axis=1)
                     )
-        whole = jnp.dot(jnp.concatenate(rows, 0), back, precision=lax.Precision.HIGHEST, preferred_element_type=F32)
+        whole = permute(jnp.concatenate(rows, 0), back)
         for s in range(2):
             for layer in range(2):
                 for side in range(2):

time: 61.8 us -> 59.7 us (0.966)
  Pallas kernels: 59.1 us -> 57.1 us
    pallas_call x1, Pallas kernels: 59.1 us -> 57.1 us  [local(): pl.pallas_call(kernel, out_shape=jax.ShapeDtypeStruct((1, 3, 2, 2, 32, 25...]
where the time goes in v3:
time: 59.7 us; the launch traced here: 59.6 us
  Pallas kernels  57.1 us (96%)
  local copies, waits for them, and re-layouts  2.49 us (4%)
    pallas_call x1, Pallas kernels, local(): pl.pallas_call(kernel, out_shape=jax.ShapeDtypeStruct((1, 3, 2, 2, 32, 25...  57.1 us
    unnamed x5, local copies, waits for them, and re-layouts  2.49 us

profile of v3, /device:TPU:128, one launch (start us, length us, event | category | flops | bytes accessed | tf_op | source)
XLA Modules:
  0.0 59.6 jit_solution(2485277837820538841)
XLA Ops:
  0.0 0.0 copy-start
  0.0 0.9 %copy-done = f32[1,2,2,32,256]{4,3,2,1,0:T(8,128)S(1)} copy-done((f32[1,2,2,32,256]{4,3,2,1,0:T(8,128)S(1)}, f32[1,2,2,32,256]{4,3,2,1,0:T(8,128)}, u32[]{:S(2)}) %copy-start) | copy-done | bytes 131096
  0.9 0.0 copy-start.1
  0.9 0.8 %copy-done.1 = f32[2,32,256]{2,1,0:T(8,128)S(1)} copy-done((f32[2,32,256]{2,1,0:T(8,128)S(1)}, f32[2,32,256]{2,1,0:T(8,128)}, u32[]{:S(2)}) %copy-start.1) | copy-done | bytes 65560
  1.7 57.1 %pfasst.1 = f32[1,3,2,2,32,256]{5,4,3,2,1,0:T(8,128)S(1)} custom-call(f32[1,2,2,32,256]{4,3,2,1,0:T(8,128)S(1)} %copy-done, f32[2,32,256]{2,1,0:T(8,128)S(1)} %copy-done.1), custom_call_target="tpu_custom_call" | custom-call | tf_op jit(solution)/shard_map/pfasst/pallas_call | solution.py:537
  58.8 0.7 %copy.4 = f32[1,3,2,2,32,256]{5,4,3,2,1,0:T(8,128)} copy(f32[1,3,2,2,32,256]{5,4,3,2,1,0:T(8,128)S(1)} %pfasst.1) | data formatting | bytes 786432
Async XLA Ops:
  0.0 0.9 %copy-start = (f32[1,2,2,32,256]{4,3,2,1,0:T(8,128)S(1)}, f32[1,2,2,32,256]{4,3,2,1,0:T(8,128)}, u32[]{:S(2)}) copy-start(f32[1,2,2,32,256]{4,3,2,1,0:T(8,128)} %init.1) | copy-start | bytes 393220
  0.9 0.8 %copy-start.1 = (f32[2,32,256]{2,1,0:T(8,128)S(1)}, f32[2,32,256]{2,1,0:T(8,128)}, u32[]{:S(2)}) copy-start(f32[2,32,256]{2,1,0:T(8,128)} %diff.1) | copy-start | bytes 196612

commit v4 on v3

--- a/solution.py
+++ b/solution.py
@@ -13,11 +13,11 @@
 W_TWO = (-0.8 / 24.0, 0.8 / 3.0, 0.8 * 5.0 / 24.0)
 
 CONSTS = (
-    (0, 0, 6), (1, 0, 4), (2, 0, 2), (3, 0, 0), (3, 3, 2), (4, 7, 8), (5, 7, 6), (6, 7, 4), (7, 7, 2), (4, 5, 4), (5, 5, 2),
+    (0, 0, 6), (1, 0, 4), (2, 0, 2), (3, 0, 0), (2, 3, 4), (3, 3, 2), (4, 7, 8), (5, 7, 6), (6, 7, 4), (7, 7, 2), (4, 5, 4), (5, 5, 2),
 )
 WIDTHS = (8, 6, 4, 2, 0)
-RUNS = {8: (7,), 6: (0, 7), 4: (0, 5, 7), 2: (0, 3, 5, 7), 0: (0,)}
-COARSE_REACH = {0: 3, 3: 2, 5: 3, 7: 5}
+RUNS = {8: (7,), 6: (0, 7), 4: (0, 3, 5, 7), 2: (0, 3, 5, 7), 0: (0,)}
+COARSE_REACH = {0: 3, 3: 3, 5: 3, 7: 5}
 MID = 10
 
 
@@ -40,8 +40,8 @@
         out |= {(t, t, j) for j in sides(reach) if abs(j) > 1}
     for src, dst, h in CONSTS:
         out |= {(src, dst, j) for j in span(h // 2 + 1) if src != dst or j}
-    out |= {(0, 3, j) for j in span(2)} | {(0, 5, j) for j in span(3)} | {(0, 7, j) for j in span(5)}
-    out |= {(0, 1, 0), (0, 2, 0), (5, 4, 0), (7, 6, 0)}
+    out |= {(0, 3, j) for j in span(3)} | {(0, 5, j) for j in span(3)} | {(0, 7, j) for j in span(5)}
+    out |= {(0, 1, 0), (3, 2, 0), (5, 4, 0), (7, 6, 0)}
     return sorted(out, key=lambda p: (p[0] != p[1] or abs(p[2]) > 1, p))
 
 
@@ -116,9 +116,9 @@
 
 
 def kernel(
-    init, diff, out, xin, din, tmp, woven, a0, a1, a2, ap, du, cd, v0, v1, r0, r1, r2, own, base, one, two,
+    init, diff, out, xin, din, tmp, woven, result, a0, a1, a2, ap, du, cd, v0, v1, r0, r1, r2, own, base, one, two,
     d8, d6, d4, d2, d0, b10, b8, b6, b4, b2, b0, w8, w6, w4, w2, w0, dummy,
-    in_sem, near_s, near_r, diff_s, diff_r, cd_s, cd_r, far_s, far_r, prev_s, prev_r, const_s, const_r, state_s, state_r, give_s, give_r,
+    in_sem, out_sem, near_s, near_r, diff_s, diff_r, cd_s, cd_r, far_s, far_r, prev_s, prev_r, const_s, const_r, state_s, state_r, give_s, give_r,
 ):
     tm = lax.axis_index("tm")
     gz = lax.axis_index("gz")
@@ -332,11 +332,7 @@
         def _(reach=reach):
             wait(cd_r, 2 * reach - 2)
 
-    @on(3)
-    def _():
-        wait(state_r, 10)
-
-    @on(5)
+    @on(3, 5)
     def _():
         wait(state_r, 14)
 
@@ -393,27 +389,22 @@
             @on(0)
             def _():
                 give(1)
-
-            @on(5, 7)
+                for j in reversed(span(3)):
+                    send(b4.at[pl.ds(4, 2)], b6.at[pl.ds(6 - 2 * j, 2)], state_s, state_r, 3, j)
+
+            @on(3, 5, 7)
             def _():
                 give(tm - 1)
-
-        if h == 2:
-            @on(0)
-            def _():
-                for j in span(2):
-                    send(b2.at[pl.ds(2, 2)], b4.at[pl.ds(4 - 2 * j, 2)], state_s, state_r, 3, j)
 
         if h == 0:
             @on(0)
             def _():
-                for j in reversed(span(5)):
+                for j in reversed(sides(5)[2:]):
                     send(b0, b10.at[pl.ds(10 - 2 * j, 2)], state_s, state_r, 7, j)
                 for j in reversed(span(3)):
                     send(b0, b6.at[pl.ds(6 - 2 * j, 2)], state_s, state_r, 5, j)
-                wait(give_s, 18)
-                for src_ref, start in ((b4, 2), (w2, 1), (b2, 0)):
-                    send(src_ref.at[pl.ds(start, 6)], src_ref.at[pl.ds(start, 6)], give_s, give_r, 2, 0)
+                for j in reversed(span(1)):
+                    send(b0, b10.at[pl.ds(10 - 2 * j, 2)], state_s, state_r, 7, j)
 
     @pl.when(tm == 0)
     def _():
@@ -447,6 +438,29 @@
     def _():
         correct(b4, 2, w2, 1, b2, 0, False)
 
+    back = swap(False)
+
+    def emit(node, ref, shift):
+        rows = []
+        for s in range(2):
+            for layer in range(2):
+                for half in range(2):
+                    rows.append(
+                        jnp.concatenate([ref[shift + layer, s, 2 * half], ref[shift + layer, s, 2 * half + 1]], axis=1)
+                    )
+        whole = permute(jnp.concatenate(rows, 0), back)
+        for s in range(2):
+            for layer in range(2):
+                for side in range(2):
+                    lanes = slice(side * 128, side * 128 + 128)
+                    for half in range(2):
+                        k = (s * 2 + layer) * 2 + half
+                        woven[node, s, layer, side, pl.ds(half, 16, stride=2), :] = whole[k * 16 : k * 16 + 16, lanes]
+                    result[node, s, layer, :, lanes] = woven[node, s, layer, side]
+        pltpu.make_async_copy(result.at[node], out.at[0, node], out_sem.at[node]).start()
+
+    emit(0, base.at[3], 2)
+
     def fourth(i):
         d = [du[i + 1, p] for p in range(4)]
         f = [fine_rate(get(base, k, i), get(base, k, i + 1), get(base, k, i + 2), d) for k in range(4)]
@@ -461,6 +475,8 @@
 
     loop(4, fourth)
 
+    emit(1, one, 1)
+
     def fifth(i):
         f = fine_rate(get(one, i), get(one, i + 1), get(one, i + 2), [du[i + 2, p] for p in range(4)])
         for s in range(2):
@@ -469,25 +485,10 @@
 
     loop(2, fifth, 2)
 
-    back = swap(False)
-    for node, (ref, shift) in enumerate(((base.at[3], 2), (one, 1), (two, 1))):
-        rows = []
-        for s in range(2):
-            for layer in range(2):
-                for half in range(2):
-                    rows.append(
-                        jnp.concatenate([ref[shift + layer, s, 2 * half], ref[shift + layer, s, 2 * half + 1]], axis=1)
-                    )
-        whole = permute(jnp.concatenate(rows, 0), back)
-        for s in range(2):
-            for layer in range(2):
-                for side in range(2):
-                    lanes = slice(side * 128, side * 128 + 128)
-                    for half in range(2):
-                        k = (s * 2 + layer) * 2 + half
-                        woven[node, s, layer, side, pl.ds(half, 16, stride=2), :] = whole[k * 16 : k * 16 + 16, lanes]
-                    out[0, node, s, layer, :, lanes] = woven[node, s, layer, side]
-
+    emit(2, two, 1)
+
+    for node in range(3):
+        pltpu.make_async_copy(result.at[node], out.at[0, node], out_sem.at[node]).wait()
     for k in range(6):
         wait(near_s.at[k], 4)
     for k in range(2):
@@ -509,9 +510,9 @@
 
     @on(0)
     def _():
-        wait(state_s, 46)
-
-    @on(0, 5, 7)
+        wait(state_s, 50)
+
+    @on(0, 3, 5, 7)
     def _():
         wait(give_s, 18)
 
@@ -523,26 +524,26 @@
     def vm(*shape):
         return pltpu.VMEM(shape, F32)
 
-    scratch = [vm(2, 2, 32, 256), vm(2, 32, 256), vm(2, 6, 32, 128), vm(3, 2, 2, 2, 32, 128)]
+    scratch = [vm(2, 2, 32, 256), vm(2, 32, 256), vm(2, 6, 32, 128), vm(3, 2, 2, 2, 32, 128), vm(3, 2, 2, 32, 256)]
     scratch += [vm(8, *fine), vm(6, *fine), vm(6, *fine), vm(6, *fine), vm(6, 4, 16, 128), vm(2 * MID + 2, 16, 128)]
     scratch += [vm(6, *coarse), vm(6, *coarse), vm(6, *coarse), vm(4, *coarse), vm(2, *coarse), vm(2, 2, *coarse)]
     scratch += [vm(4, 6, *fine), vm(4, *fine), vm(4, *fine)]
     scratch += [vm(2 * h + 4, 2, *coarse) for h in WIDTHS]
     scratch += [vm(2 * h + 2, *coarse) for h in (10,) + WIDTHS]
     scratch += [vm(2 * h + 4, *coarse) for h in WIDTHS]
-    scratch += [vm(48, *coarse)]
+    scratch += [vm(52, *coarse)]
     dma = pltpu.SemaphoreType.DMA
     one = [dma(()), dma(())]
-    scratch += [dma((2,)), dma((6,)), dma((6,)), dma((2,)), dma((2,))] + one * 3 + [dma((len(CONSTS),)), dma((5,))] + one * 2
+    scratch += [dma((2,)), dma((3,)), dma((6,)), dma((6,)), dma((2,)), dma((2,))] + one * 3 + [dma((len(CONSTS),)), dma((5,))] + one * 2
     return pl.pallas_call(
         kernel,
         out_shape=jax.ShapeDtypeStruct((1, 3, 2, 2, 32, 256), F32),
         in_specs=[pl.BlockSpec(memory_space=pltpu.HBM)] * 2,
-        out_specs=pl.BlockSpec(memory_space=pltpu.VMEM),
+        out_specs=pl.BlockSpec(memory_space=pl.ANY),
         scratch_shapes=scratch,
         name="pfasst",
         compiler_params=pltpu.CompilerParams(
-            collective_id=0, has_side_effects=True, vmem_limit_bytes=32 * 1024 * 1024
+            collective_id=0, has_side_effects=True, vmem_limit_bytes=60 * 1024 * 1024
         ),
     )(init_states, diffusivity)
 

time: 59.7 us -> 59.5 us (level)
  local copies, waits for them, and re-layouts: 2.49 us -> 1.77 us
    unnamed x5 -> x1, local copies, waits for them, and re-layouts: 2.49 us -> 1.77 us
where the time goes in v4:
time: 59.5 us; the launch traced here: 59.2 us
  Pallas kernels  57.5 us (97%)
  local copies, waits for them, and re-layouts  1.77 us (3%)
    pallas_call x1, Pallas kernels, local(): pl.pallas_call(kernel, out_shape=jax.ShapeDtypeStruct((1, 3, 2, 2, 32, 25...  57.5 us
    unnamed x1, local copies, waits for them, and re-layouts  1.77 us

profile of v4, /device:TPU:128, one launch (start us, length us, event | category | flops | bytes accessed | tf_op | source)
XLA Modules:
  0.0 59.2 jit_solution(16663332196336487404)
XLA Ops:
  0.0 57.5 %pfasst.1 = f32[1,3,2,2,32,256]{5,4,3,2,1,0:T(8,128)} custom-call(f32[1,2,2,32,256]{4,3,2,1,0:T(8,128)} %init.1, f32[2,32,256]{2,1,0:T(8,128)} %diff.1), custom_call_target="tpu_custom_call" | custom-call | tf_op jit(solution)/shard_map/pfasst/pallas_call | solution.py:538
  57.5 1.8 %copy.4 = f32[1,3,2,2,32,256]{5,4,3,2,1,0:T(8,128)} copy(f32[1,3,2,2,32,256]{5,4,3,2,1,0:T(8,128)} %pfasst.1) | data formatting | bytes 786432

commit v5 on v4

--- a/solution.py
+++ b/solution.py
@@ -93,7 +93,10 @@
             body(k * chunk + i)
         return carry
 
-    lax.fori_loop(0, count // chunk, many, 0)
+    if count == chunk:
+        many(0, 0)
+    else:
+        lax.fori_loop(0, count // chunk, many, 0)
 
 
 def swap(forward):
@@ -278,8 +281,8 @@
                 send(own.at[1, 0], ref.at[0, 0], *sems, dst, j)
                 send(own.at[0, 0], ref.at[2 * h + 3, 0], *sems, dst, -j)
 
+    share()
     spread((5, 7))
-    share()
     send(a2.at[2], a2.at[0], far_s, far_r, tm, 1)
     send(a2.at[3], a2.at[5], far_s, far_r, tm, -1)
 
@@ -342,6 +345,10 @@
 
     chunks = {20: 10, 18: 9, 16: 8, 14: 7, 12: 6, 10: 10, 8: 8, 6: 6, 4: 4, 2: 2}
 
+    def give(node, dst):
+        src, start, ref, to = ((b6, 4, b4, 2), (w4, 3, w2, 1), (b4, 2, b2, 0))[node]
+        send(src.at[pl.ds(start, 6)], ref.at[pl.ds(to, 6)], give_s, give_r, dst, 0)
+
     for h in WIDTHS:
         begin, mid, end, e = state[h + 2], middle[h], state[h], const[h]
 
@@ -377,24 +384,27 @@
                     loop(2 * h + 4, half, chunks[2 * h + 4])
             else:
                 loop(2 * h + 4, half, chunks[2 * h + 4])
+            if h == 4:
+                for node in range(2):
+                    @pl.when(tm == 0)
+                    def _(node=node):
+                        give(node, 1)
+
+                    @pl.when(tm > 0)
+                    def _(node=node):
+                        give(node, tm - 1)
             loop(2 * h + 2, full, chunks[2 * h + 2])
-
-        def give(dst):
-            for k, (src_ref, start, dst_ref, to) in enumerate(
-                ((state[h + 2], h, b4, 2), (middle[h], h - 1, w2, 1), (state[h], h - 2, b2, 0))
-            ):
-                send(src_ref.at[pl.ds(start, 6)], dst_ref.at[pl.ds(to, 6)], give_s, give_r, dst, 0)
 
         if h == 4:
             @on(0)
             def _():
-                give(1)
+                give(2, 1)
                 for j in reversed(span(3)):
                     send(b4.at[pl.ds(4, 2)], b6.at[pl.ds(6 - 2 * j, 2)], state_s, state_r, 3, j)
 
             @on(3, 5, 7)
             def _():
-                give(tm - 1)
+                give(2, tm - 1)
 
         if h == 0:
             @on(0)
@@ -428,7 +438,7 @@
                             else:
                                 base[3, i, s, p] = base[3, i, s, p] + w
 
-        loop(6, body)
+        loop(6, body, 2)
 
     @pl.when(tm == 0)
     def _():
@@ -459,8 +469,6 @@
                     result[node, s, layer, :, lanes] = woven[node, s, layer, side]
         pltpu.make_async_copy(result.at[node], out.at[0, node], out_sem.at[node]).start()
 
-    emit(0, base.at[3], 2)
-
     def fourth(i):
         d = [du[i + 1, p] for p in range(4)]
         f = [fine_rate(get(base, k, i), get(base, k, i + 1), get(base, k, i + 2), d) for k in range(4)]
@@ -473,9 +481,7 @@
                 one[i, s, p] = b_one
                 two[i, s, p] = b_one - STEP * rates[1] + i_two
 
-    loop(4, fourth)
-
-    emit(1, one, 1)
+    loop(4, fourth, 2)
 
     def fifth(i):
         f = fine_rate(get(one, i), get(one, i + 1), get(one, i + 2), [du[i + 2, p] for p in range(4)])
@@ -485,6 +491,8 @@
 
     loop(2, fifth, 2)
 
+    emit(0, base.at[3], 2)
+    emit(1, one, 1)
     emit(2, two, 1)
 
     for node in range(3):

time: 59.5 us -> 58.8 us (0.988)
  the two profiles are of different devices: /device:TPU:128 before, /device:TPU:192 now
where the time goes in v5:
time: 58.8 us; the launch traced here: 58.6 us
  Pallas kernels  56.8 us (97%)
  local copies, waits for them, and re-layouts  1.77 us (3%)
    pallas_call x1, Pallas kernels, local(): pl.pallas_call(kernel, out_shape=jax.ShapeDtypeStruct((1, 3, 2, 2, 32, 25...  56.8 us
    unnamed x1, local copies, waits for them, and re-layouts  1.77 us

profile of v5, /device:TPU:192, one launch (start us, length us, event | category | flops | bytes accessed | tf_op | source)
XLA Modules:
  0.0 58.6 jit_solution(6083008030917430683)
XLA Ops:
  0.0 56.8 %pfasst.1 = f32[1,3,2,2,32,256]{5,4,3,2,1,0:T(8,128)} custom-call(f32[1,2,2,32,256]{4,3,2,1,0:T(8,128)} %init.1, f32[2,32,256]{2,1,0:T(8,128)} %diff.1), custom_call_target="tpu_custom_call" | custom-call | tf_op jit(solution)/shard_map/pfasst/pallas_call | solution.py:546
  56.9 1.8 %copy.4 = f32[1,3,2,2,32,256]{5,4,3,2,1,0:T(8,128)} copy(f32[1,3,2,2,32,256]{5,4,3,2,1,0:T(8,128)} %pfasst.1) | data formatting | bytes 786432

commit v6 on v5

--- a/solution.py
+++ b/solution.py
@@ -481,7 +481,7 @@
                 one[i, s, p] = b_one
                 two[i, s, p] = b_one - STEP * rates[1] + i_two
 
-    loop(4, fourth, 2)
+    loop(4, fourth, 4)
 
     def fifth(i):
         f = fine_rate(get(one, i), get(one, i + 1), get(one, i + 2), [du[i + 2, p] for p in range(4)])

time: 58.8 us -> 58.7 us (level)
  no operation moved by 1% of the time
where the time goes in v6:
time: 58.7 us; the launch traced here: 58.5 us
  Pallas kernels  56.7 us (97%)
  local copies, waits for them, and re-layouts  1.77 us (3%)
    pallas_call x1, Pallas kernels, local(): pl.pallas_call(kernel, out_shape=jax.ShapeDtypeStruct((1, 3, 2, 2, 32, 25...  56.7 us
    unnamed x1, local copies, waits for them, and re-layouts  1.77 us

profile of v6, /device:TPU:192, one launch (start us, length us, event | category | flops | bytes accessed | tf_op | source)
XLA Modules:
  0.0 58.5 jit_solution(1712314773251374826)
XLA Ops:
  0.0 56.7 %pfasst.1 = f32[1,3,2,2,32,256]{5,4,3,2,1,0:T(8,128)} custom-call(f32[1,2,2,32,256]{4,3,2,1,0:T(8,128)} %init.1, f32[2,32,256]{2,1,0:T(8,128)} %diff.1), custom_call_target="tpu_custom_call" | custom-call | tf_op jit(solution)/shard_map/pfasst/pallas_call | solution.py:546
  56.8 1.8 %copy.4 = f32[1,3,2,2,32,256]{5,4,3,2,1,0:T(8,128)} copy(f32[1,3,2,2,32,256]{5,4,3,2,1,0:T(8,128)} %pfasst.1) | data formatting | bytes 786432
